TPU v7x, 256 devices: a whole 4x4x8 slice. The times are simulated.
256 devices in a mesh: tile: 64 (over y, x, z_lo), agg: 4 (over z_hi, core).
Axes of the slice: x: 4, y: 4, z: 8 (z_hi: 2, z_lo: 4; z = z_hi * 4 + z_lo), core: 2. Of those that a mesh axis runs over, the one named last changes fastest.
Arguments:
- a_blocks: bfloat16 [4096, 6, 4096], P(('tile', 'agg')), may hold values from -0.75 to 0.75
- p_blocks: bfloat16 [4096, 4096], P(('tile', 'agg')), may hold values from -0.75 to 0.75
- columns: int32 [4096, 6], P(('tile', 'agg')), may hold values from 0 to 4095, as said below
- agg_ids: int32 [4096], replicated, may hold values from 0 to 1637, never falling along the last dimension, each value on 1 to 4 neighbouring positions
Outputs:
- coarse: bfloat16 [4096, 7, 4096], P('tile')
Inputs may be any that keep to these rules, and one draw needn't show every extreme that they name: `columns`: each row's first entry is the row itself; the others are block rows other than itself within 3 of it, distinct except in the first and last 3 rows, where a column may be named twice. `agg_ids`: starts at 0, never falls, rises by at most 1 from row to row; each aggregate has 1 to 4 rows.
All inputs are finite; a program needn't handle non-finite values.
Results may differ from a plain program's by a relative error of at most 0.015.
Values may be sent and summed in bfloat16 or wider, within the bound.
A program may use at most 64 MiB of HBM per device.

v0:
```python
import jax
import jax.numpy as jnp
from jax import lax
from jax.sharding import PartitionSpec as P

BS = 64
NNZB = 6
REACH = 3
BAND = 7


def extended(cells, sides, width):
    for axis, dim in sides:
        count = lax.axis_size(axis)
        ends = count - 1
        head = lax.slice_in_dim(cells, 0, width, axis=dim)
        tail = lax.slice_in_dim(cells, cells.shape[dim] - width, cells.shape[dim], axis=dim)
        cells = jnp.concatenate(
            [
                lax.ppermute(tail, axis, [(i, (i + 1) % count) for i in range(ends)]),
                cells,
                lax.ppermute(head, axis, [((i + 1) % count, i) for i in range(ends)]),
            ],
            axis=dim,
        )
    return cells


def shifted(block, axis, distance):
    devices = range(lax.axis_size(axis))
    route = [(i - distance, i) for i in devices if i - distance in devices]
    return lax.ppermute(block, axis, route)


def block_starts(agg_ids):
    count = agg_ids.shape[0]
    place = jnp.arange(count, dtype=jnp.int32)
    fresh = jnp.concatenate([jnp.ones((1,), dtype=bool), agg_ids[1:] != agg_ids[:-1]])
    return lax.cummax(jnp.where(fresh, place, 0), axis=0)


def local(a_blocks, p_blocks, columns, agg_ids):
    blocks = p_blocks.shape[0]
    rank = lax.axis_index(("tile", "agg"))
    base = rank * blocks
    padded = extended(p_blocks, ((("tile", "agg"), 0),), REACH)
    first = block_starts(agg_ids)
    own_ids = lax.dynamic_slice_in_dim(agg_ids, base, blocks, 0)
    own_first = lax.dynamic_slice_in_dim(first, base, blocks, 0)
    offsets = agg_ids[columns] - own_ids[:, None] + REACH
    picked = padded[columns - base + REACH].reshape(blocks, NNZB, BS, BS)
    amat = a_blocks.reshape(blocks, NNZB, BS, BS)
    prods = jnp.einsum("ikpq,ikqr->ikpr", amat, picked, preferred_element_type=jnp.float32)
    select = (offsets[..., None] == jnp.arange(BAND, dtype=jnp.int32)).astype(jnp.float32)
    band_rows = jnp.einsum("iko,ikpr->iopr", select, prods).astype(jnp.bfloat16)
    own = p_blocks.reshape(blocks, BS, BS)
    terms = jnp.einsum("iqp,ioqr->iopr", own, band_rows, preferred_element_type=jnp.float32)
    target = own_first - base
    assign = (target[None, :] == jnp.arange(blocks, dtype=jnp.int32)[:, None]).astype(jnp.float32)
    rows = jnp.einsum("ri,iopq->ropq", assign, terms)
    outside = (target < 0).astype(jnp.float32)
    leading = jnp.einsum("i,iopq->opq", outside, terms)
    incoming = shifted(leading, ("tile", "agg"), -1)
    last_target = first[base + blocks - 1] - base
    marker = (jnp.arange(blocks, dtype=jnp.int32) == last_target).astype(jnp.float32)
    rows = rows + marker[:, None, None, None] * incoming[None]
    finished = rows.astype(jnp.bfloat16).reshape(blocks, BAND, BS * BS)
    return lax.all_gather(finished, "agg", axis=0, tiled=True)


def solution(mesh):
    return jax.shard_map(
        local,
        mesh=mesh,
        in_specs=(
            P(("tile", "agg"), None, None),
            P(("tile", "agg"), None),
            P(("tile", "agg"), None),
            P(),
        ),
        out_specs=P("tile", None, None),
        check_vma=False,
    )
```

profile of v0, /device:TPU:1, one launch (start us, length us, event | category | flops | bytes accessed | tf_op | source)
XLA Modules:
  0.0 135.1 jit_solution(1944475080450721261)
XLA Ops:
  6.5 0.0 copy-start
  6.5 0.0 all-gather.2.cloned.1.call-start
  6.5 0.9 fusion.18
  7.5 10.2 %collective-permute-start = (bf16[3,4096]{1,0:T(4,128)(2,1)S(1)}, bf16[3,4096]{1,0:T(4,128)(2,1)S(1)}, u32[]{:S(2)}, u32[]{:S(2)}) collective-permute-start(bf16[3,4096]{1,0:T(4,128)(2,1)S(1)} %get-tuple-element.5), channel_id=1, source_target_pairs={{0,1},{1,2},{2,3},{3,4},{4,5},{5,6},{6,7},{7,8},{8,9},{9,10},{10,1... | collective-permute-start | bytes 73736 | tf_op jit(solution)/shard_map/ppermute | solution.py:20
  17.7 1.9 %collective-permute-start.1 = (bf16[3,4096]{1,0:T(4,128)(2,1)S(1)}, bf16[3,4096]{1,0:T(4,128)(2,1)S(1)}, u32[]{:S(2)}, u32[]{:S(2)}) collective-permute-start(bf16[3,4096]{1,0:T(4,128)(2,1)S(1)} %get-tuple-element.6), channel_id=1, source_target_pairs={{1,0},{2,1},{3,2},{4,3},{5,4},{6,5},{7,6},{8,7},{9,8},{10,9},{11,1... | collective-permute-start | bytes 73736 | tf_op jit(solution)/shard_map/ppermute | solution.py:22
  19.6 0.9 slice_compare_fusion
  20.5 0.8 dynamic_slice.10
  21.2 0.8 copy.10
  22.0 0.1 reshape.60
  22.1 0.1 reshape.68
  22.2 0.0 copy-done
  22.2 0.0 copy-start.1
  22.2 0.0 copy-start.2
  22.2 1.1 gather_fusion
  23.4 0.1 reshape.59
  23.5 0.1 add_select_fusion
  23.6 0.3 reduce-window.9
  23.9 0.1 slice.29
  23.9 0.1 reduce-window.12
  24.0 0.1 slice_reduce_fusion
  24.1 0.1 maximum_bitcast_fusion
  24.2 0.1 subtract_add_fusion
  24.2 0.1 dynamic-slice_subtract_fusion
  24.3 0.0 copy-done.1
  24.3 0.2 reshape.80
  24.6 0.0 copy-done.2
  24.6 1.7 %reshape.55 = bf16[16,6,64,64]{3,2,0,1:T(8,128)(2,1)S(1)} reshape(bf16[16,6,4096]{2,0,1:T(8,128)(2,1)S(1)} %copy-done.2) | data formatting | bytes 1572864 | tf_op jit(solution)/shard_map/reshape | solution.py:52
  26.3 0.0 collective-permute-done
  26.3 0.5 collective-permute-done.1
  26.8 0.1 pad_maximum_fusion
  26.9 1.9 %gather_fusion.1 = bf16[96,4096]{1,0:T(8,128)(2,1)} fusion(bf16[22,4096]{1,0:T(8,128)(2,1)S(1)} %pad_maximum_fusion, s32[1024]{0:T(1024)S(1)} %pad_clamp_fusion), kind=kCustom, calls=%fused_computation.1 | custom fusion | bytes 1573248 | tf_op jit(solution)/shard_map/gather | solution.py:51
  28.8 2.5 %reshape.54 = bf16[16,6,64,64]{3,2,1,0:T(8,128)(2,1)S(1)} reshape(bf16[96,4096]{1,0:T(8,128)(2,1)} %gather_fusion.1) | data formatting | bytes 1572864 | tf_op jit(solution)/shard_map/reshape | solution.py:51
  31.3 2.1 %convolution_bitcast_fusion.1 = bf16[16,6,64,64]{2,3,1,0:T(8,128)(2,1)} fusion(bf16[16,6,64,64]{3,2,1,0:T(8,128)(2,1)S(1)} %reshape.54, bf16[16,6,64,64]{3,2,0,1:T(8,128)(2,1)S(1)} %reshape.55), kind=kOutput, calls=%fused_computation.4 | convolution fusion | flops 50331648 | bytes 2359296 | tf_op jit(solution)/shard_map/ikpq,ikqr->ikpr/dot_general | solution.py:53
  33.5 3.1 %copy.18 = bf16[16,6,64,64]{3,1,2,0:T(8,128)(2,1)S(1)} copy(bf16[16,6,64,64]{2,3,1,0:T(8,128)(2,1)} %convolution_bitcast_fusion.1) | data formatting | bytes 1572864 | tf_op jit(solution)/shard_map/ikpq,ikqr->ikpr/dot_general | solution.py:53
  36.6 2.3 %fusion.4 = bf16[16,7,64,64]{3,1,2,0:T(8,128)(2,1)} fusion(bf16[16,6,64,64]{3,1,2,0:T(8,128)(2,1)S(1)} %copy.18, s32[16,6]{1,0:T(8,128)S(1)} %subtract_add_fusion), kind=kOutput, calls=%fused_computation.11 | convolution fusion | flops 5505696 | bytes 1704320 | tf_op jit(solution)/shard_map/iko,ikpr->iopr/dot_general | solution.py:55
  38.9 3.4 %copy.19 = bf16[16,7,64,64]{2,3,1,0:T(8,128)(2,1)S(1)} copy(bf16[16,7,64,64]{3,1,2,0:T(8,128)(2,1)} %fusion.4) | data formatting | bytes 1835008 | tf_op jit(solution)/shard_map/iko,ikpr->iopr/dot_general | solution.py:55
  42.3 1.8 %convolution_bitcast_fusion = bf16[16,7,64,64]{2,3,1,0:T(8,128)(2,1)} fusion(bf16[16,7,64,64]{2,3,1,0:T(8,128)(2,1)S(1)} %copy.19, bf16[16,64,64,1]{2,1,0,3:T(8,128)(2,1)S(1)} %reshape.80), kind=kOutput, calls=%fused_computation.3 | convolution fusion | flops 58720256 | bytes 1966080 | tf_op jit(solution)/shard_map/iqp,ioqr->iopr/dot_general | solution.py:57
  44.1 3.5 %copy.14 = bf16[16,7,64,64]{3,0,2,1:T(8,128)(2,1)S(1)} copy(bf16[16,7,64,64]{2,3,1,0:T(8,128)(2,1)} %convolution_bitcast_fusion) | data formatting | bytes 1835008 | tf_op jit(solution)/shard_map/iqp,ioqr->iopr/transpose | solution.py:57
  47.6 0.4 fusion.13
  48.0 1.9 %collective-permute-start.2 = (f32[7,64,64]{2,1,0:T(8,128)S(1)}, f32[7,64,64]{2,1,0:T(8,128)S(1)}, u32[]{:S(2)}, u32[]{:S(2)}) collective-permute-start(f32[7,64,64]{2,1,0:T(8,128)S(1)} %bitcast.44), channel_id=1, source_target_pairs={{1,0},{2,1},{3,2},{4,3},{5,4},{6,5},{7,6},{8,7},{9,8},{10,9},{11,1... | collective-permute-start | bytes 344072 | tf_op jit(solution)/shard_map/ppermute | solution.py:32
  49.9 0.6 dynamic_slice.11
  51.2 12.3 %collective-permute-done.2 = f32[7,64,64]{2,1,0:T(8,128)S(1)} collective-permute-done((f32[7,64,64]{2,1,0:T(8,128)S(1)}, f32[7,64,64]{2,1,0:T(8,128)S(1)}, u32[]{:S(2)}, u32[]{:S(2)}) %collective-permute-start.2) | collective-permute-done | bytes 114720 | tf_op jit(solution)/shard_map/ppermute | solution.py:32
  63.5 0.6 add_convert_fusion
  64.1 0.5 copy.15
  64.6 2.3 %reshape.57 = bf16[16,7,4096]{2,0,1:T(8,128)(2,1)} reshape(bf16[16,7,64,64]{3,2,0,1:T(8,128)(2,1)S(1)} %copy.15) | data formatting | bytes 1835008 | tf_op jit(solution)/shard_map/reshape | solution.py:67
  66.9 0.0 all-gather.2.cloned.1.call-update
  66.9 57.1 %all-gather.2.cloned.1.call-done = bf16[64,7,4096]{2,0,1:T(8,128)(2,1)} async-done(((bf16[16,7,4096]{2,0,1:T(8,128)(2,1)}), bf16[64,7,4096]{2,0,1:T(8,128)(2,1)}) %all-gather.2.cloned.1.call-update) | async-done | bytes 3670032 | tf_op jit(solution)/shard_map/all_gather | solution.py:68
  124.0 4.3 %copy.27 = bf16[64,7,4096]{2,0,1:T(8,128)(2,1)} copy(bf16[64,7,4096]{2,0,1:T(8,128)(2,1)} %all-gather.2.cloned.1.call-done) | data formatting | bytes 7340032
  (4 shorter events, 0.0 us)
Async XLA Ops:
  6.5 15.7 %copy-start = (s32[4096]{0:T(1024)S(1)}, s32[4096]{0:T(1024)}, u32[]{:S(2)}) copy-start(s32[4096]{0:T(1024)} %param.7) | copy-start | bytes 49156
  6.5 117.5 %all-gather.2.cloned.1.call-start = ((), (), s32[]{:S(2)}) async-start(), calls=%async_computation | async-start | bytes 4587520 | tf_op jit(solution)/shard_map/all_gather | solution.py:68
  7.5 18.9 %collective-permute-start = (bf16[3,4096]{1,0:T(4,128)(2,1)S(1)}, bf16[3,4096]{1,0:T(4,128)(2,1)S(1)}, u32[]{:S(2)}, u32[]{:S(2)}) collective-permute-start(bf16[3,4096]{1,0:T(4,128)(2,1)S(1)} %get-tuple-element.5), channel_id=1, source_target_pairs={{0,1},{1,2},{2,3},{3,4},{4,5},{5,6},{6,7},{7,8},{8,9},{9,10},{10,1... | collective-permute-start | bytes 73736 | tf_op jit(solution)/shard_map/ppermute | solution.py:20
  17.7 9.1 %collective-permute-start.1 = (bf16[3,4096]{1,0:T(4,128)(2,1)S(1)}, bf16[3,4096]{1,0:T(4,128)(2,1)S(1)}, u32[]{:S(2)}, u32[]{:S(2)}) collective-permute-start(bf16[3,4096]{1,0:T(4,128)(2,1)S(1)} %get-tuple-element.6), channel_id=1, source_target_pairs={{1,0},{2,1},{3,2},{4,3},{5,4},{6,5},{7,6},{8,7},{9,8},{10,9},{11,1... | collective-permute-start | bytes 73736 | tf_op jit(solution)/shard_map/ppermute | solution.py:22
  22.2 2.1 %copy-start.1 = (bf16[16,4096]{1,0:T(8,128)(2,1)S(1)}, bf16[16,4096]{1,0:T(8,128)(2,1)}, u32[]{:S(2)}) copy-start(bf16[16,4096]{1,0:T(8,128)(2,1)} %param.5) | copy-start | bytes 393220
  22.2 2.4 %copy-start.2 = (bf16[16,6,4096]{2,0,1:T(8,128)(2,1)S(1)}, bf16[16,6,4096]{2,0,1:T(8,128)(2,1)}, u32[]{:S(2)}) copy-start(bf16[16,6,4096]{2,0,1:T(8,128)(2,1)} %param.4) | copy-start | bytes 2359300
  48.0 15.5 %collective-permute-start.2 = (f32[7,64,64]{2,1,0:T(8,128)S(1)}, f32[7,64,64]{2,1,0:T(8,128)S(1)}, u32[]{:S(2)}, u32[]{:S(2)}) collective-permute-start(f32[7,64,64]{2,1,0:T(8,128)S(1)} %bitcast.44), channel_id=1, source_target_pairs={{1,0},{2,1},{3,2},{4,3},{5,4},{6,5},{7,6},{8,7},{9,8},{10,9},{11,1... | collective-permute-start | bytes 344072 | tf_op jit(solution)/shard_map/ppermute | solution.py:32
Sparse Core Ops, SparseCore 0:
  67.0 56.9 all-gather.1
where the time goes:
time: 136 us; the launch traced here: 135 us
  waiting for transfers between devices  69.9 us (51%)
  local copies, waits for them, and re-layouts  28 us (21%)
  between operations  14.2 us (10%)
  starting transfers between devices  14.1 us (10%)
  matrix products  7.29 us (5%)
  other arithmetic  1.63 us (1%)
    all_gather x1, waiting for transfers between devices, local(): return lax.all_gather(finished, 'agg', axis=0, tiled=True)  57.1 us
    ppermute x1, waiting for transfers between devices, shifted(): return lax.ppermute(block, axis, route)  12.3 us
    ppermute x1, starting transfers between devices, extended(): lax.ppermute(tail, axis, [(i, (i + 1) % count) for i in range(ends)])  10.2 us
    unnamed x8, local copies, waits for them, and re-layouts  5.07 us
    transpose x1, local copies, waits for them, and re-layouts, local(): jnp.einsum('iqp,ioqr->iopr', own, band_rows, preferred_element_type=jnp.f...  3.48 us
    dot_general x1, local copies, waits for them, and re-layouts, local(): band_rows = jnp.einsum('iko,ikpr->iopr', select, prods).astype(jnp.bfloat16)  3.37 us
    dot_general x1, local copies, waits for them, and re-layouts, local(): jnp.einsum('ikpq,ikqr->ikpr', amat, picked, preferred_element_type=jnp.fl...  3.11 us
  transfers between devices with their start and end apart: 4, of which 3 were waited for; matrix products, arithmetic and copies ran while one was open for 5% of the time, Pallas kernels for 0%

commit v1 on v0

v1 whole, which is shorter than its diff:
```python
import functools

import jax
import jax.numpy as jnp
from jax import lax
from jax.experimental import pallas as pl
from jax.experimental.pallas import tpu as pltpu
from jax.sharding import PartitionSpec as P

MESH = pl.DeviceIdType.MESH
BS = 64
NNZB = 6
REACH = 3
BAND = 7
ROWS = 16
NB = 4096
Q = 32
F32 = jnp.float32
BF16 = jnp.bfloat16


def dot(x, y):
    return lax.dot_general(x, y, (((1,), (0,)), ((), ())), preferred_element_type=F32)


def dot_nt(x, y):
    return lax.dot_general(x, y, (((1,), (1,)), ((), ())), preferred_element_type=F32)


def iota(shape, dim):
    return lax.broadcasted_iota(jnp.int32, shape, dim)


def segment(ids, g):
    last = NB - 1
    own = ids[g]
    start = jnp.logical_or(g == 0, ids[jnp.maximum(g - 1, 0)] != own)
    length = jnp.int32(1)
    for step in range(1, 4):
        same = jnp.logical_and(g + step <= last, ids[jnp.minimum(g + step, last)] == own)
        length = length + same.astype(jnp.int32)
    low = ids[jnp.maximum(g - REACH, 0)] - own + REACH
    high = ids[jnp.minimum(g + length - 1 + REACH, last)] - own + REACH
    return start, low, high, length


def kernel(K, ids, cols, a_ref, p_ref, out_ref, pscr, p2, hl, hr, dmat, lmat, ascr, blk, lead_out, lead_in, wire, wf, pk, sel, tab, ssem, rsem):
    t = lax.axis_index("tile")
    a = lax.axis_index("agg")
    rank = t * 4 + a
    base = rank * ROWS
    ranks = NB // ROWS
    nxt = lax.rem(rank + 1, ranks)
    prv = lax.rem(rank + ranks - 1, ranks)
    dev = lambda r: (r // 4, lax.rem(r, 4))
    sib = (t, a + 1 - 2 * lax.rem(a, 2))
    par = (t, lax.rem(a + 2, 4))
    bar = pltpu.get_barrier_semaphore()
    for d in (dev(nxt), dev(prv), sib, par):
        pl.semaphore_signal(bar, inc=1, device_id=d, device_id_type=MESH)

    pf = p_ref[...].astype(F32)
    for q in range(Q):
        pscr[pl.ds(q * ROWS, ROWS), :] = pf[:, q * 128:(q + 1) * 128]
    for i in range(ROWS):
        p2[pl.ds(i * Q, Q), :] = pscr[pl.ds(i, Q, stride=ROWS), :].astype(BF16)
    pl.semaphore_wait(bar, 4)

    def copy(src, dst, n, to):
        return pltpu.make_async_remote_copy(src_ref=src, dst_ref=dst, send_sem=ssem.at[n], recv_sem=rsem.at[n], device_id=to, device_id_type=MESH)

    H = REACH * Q
    c_right = copy(p2.at[pl.ds((ROWS - REACH) * Q, H)], hl, 0, dev(nxt))
    c_left = copy(p2.at[pl.ds(0, H)], hr, 1, dev(prv))
    c_right.start()
    c_left.start()

    r_, c_ = iota((128, 64), 0), iota((128, 64), 1)
    cc = lax.rem(r_, 64)
    flip = (lax.rem(cc, 2) != r_ // 64).astype(jnp.int32)
    spread = (c_ == cc // 2 + 32 * flip).astype(F32).astype(BF16)
    r2, l2 = iota((128, 128), 0), iota((128, 128), 1)
    diag = (r2 // 64) == (l2 // 64)
    low = iota((Q, 128), 1) < 64

    def spread_block(blockf):
        both = jnp.concatenate([blockf, pltpu.roll(blockf, 64, 1)], axis=0).astype(BF16)
        return jnp.where(diag, dot(spread, both), 0.0).astype(BF16)

    pr, pc = iota((64, 128), 0), iota((64, 128), 1)
    order = jnp.where(pr < 32, 2 * pr, 2 * (pr - 32) + 1)
    perm = (lax.rem(pc, 64) == order).astype(F32).astype(BF16)
    for i in range(ROWS):
        bf = p2[pl.ds(i * Q, Q), :].astype(F32)
        dmat[i + REACH] = spread_block(bf)
        split = jnp.concatenate([jnp.where(low, bf, 0.0), jnp.where(low, 0.0, bf)], axis=0).astype(BF16)
        lmat[pl.ds(i * 64, 64), :] = dot_nt(perm, split).astype(BF16)

    c_right.wait()
    c_left.wait()
    for i in range(REACH):
        dmat[i] = spread_block(hl[pl.ds(i * Q, Q), :].astype(F32))
        dmat[i + REACH + ROWS] = spread_block(hr[pl.ds(i * Q, Q), :].astype(F32))

    for k in range(NNZB):
        x = a_ref[k].astype(F32)
        for q in range(Q):
            ascr[pl.ds(k * 512 + q * ROWS, ROWS), :] = x[:, q * 128:(q + 1) * 128]

    acc = None
    for i in range(ROWS):
        own = ids[base + i]
        bands = [jnp.zeros((Q, 128), F32)] * 8
        for k in range(NNZB):
            a2 = ascr[pl.ds(k * 512 + i, Q, stride=ROWS), :].astype(BF16)
            j = cols[k, i]
            prod = dot(a2, dmat[jnp.clip(j - base + REACH, 0, ROWS + 2 * REACH - 1)])
            o = ids[j] - own + REACH
            for b in range(BAND):
                bands[b] = bands[b] + jnp.where(o == b, 1.0, 0.0).astype(F32) * prod
        ev, od = [], []
        for m in range(4):
            x0, x1 = bands[2 * m], bands[2 * m + 1]
            ev.append(jnp.where(low, x0, pltpu.roll(x1, 64, 1)))
            od.append(jnp.where(low, pltpu.roll(x0, 64, 1), x1))
        bcat = jnp.concatenate([jnp.concatenate(ev, axis=1), jnp.concatenate(od, axis=1)], axis=0).astype(BF16)
        term = dot(lmat[pl.ds(i * 64, 64), :], bcat)
        if acc is None:
            acc = term
        else:
            keep = jnp.where(ids[base + i - 1] == own, 1.0, 0.0).astype(F32)
            acc = term + keep * acc
        for m in range(4):
            x0, y0 = acc[:Q, m * 128:(m + 1) * 128], acc[Q:, m * 128:(m + 1) * 128]
            blk[i * 8 + 2 * m] = jnp.where(low, x0, pltpu.roll(y0, 64, 1))
            if m < 3:
                blk[i * 8 + 2 * m + 1] = jnp.where(low, pltpu.roll(x0, 64, 1), y0)
            else:
                blk[i * 8 + 7] = jnp.zeros((Q, 128), F32)
    blk[ROWS * 8] = jnp.zeros((Q, 128), F32)

    leads = jnp.where(jnp.logical_and(base > 0, ids[jnp.maximum(base - 1, 0)] == ids[base]), 1.0, 0.0).astype(F32)
    e = jnp.int32(0)
    run = jnp.int32(1)
    for step in range(1, 3):
        run = run * (ids[base + step] == ids[base]).astype(jnp.int32)
        e = e + run
    for o in range(BAND):
        lead_out[pl.ds(o * Q, Q), :] = (leads * blk[e * 8 + o]).astype(BF16)
    c_lead = copy(lead_out, lead_in, 2, dev(prv))
    c_lead.start()

    after = jnp.int32(ROWS)
    tab[0, ROWS], tab[1, ROWS], tab[2, ROWS], tab[3, ROWS] = jnp.int32(0), jnp.int32(1 << 20), jnp.int32(ROWS), jnp.int32(ROWS)
    for i in range(ROWS - 1, -1, -1):
        start, lo, hi, length = segment(ids, base + i)
        tab[0, i] = lo
        tab[1, i] = hi
        tab[2, i] = jnp.minimum(i + length - 1, ROWS - 1)
        tab[3, i] = after
        after = jnp.where(start, i, after)

    c_lead.wait()
    for o in range(BAND):
        at = (ROWS - 1) * 8 + o
        blk[at] = blk[at] + lead_in[pl.ds(o * Q, Q), :].astype(F32)

    s, o = after, tab[0, after]
    for m in range(K):
        at = jnp.minimum(tab[2, s] * 8 + o, ROWS * 8)
        wf[pl.ds(m, Q, stride=K), :] = blk[at]
        more = o < tab[1, s]
        s2 = jnp.where(more, s, tab[3, s])
        o = jnp.where(more, o + 1, tab[0, s2])
        s = s2
    wire[...] = wf[...].astype(BF16)

    c_sib = copy(wire, pk.at[0], 3, sib)
    c_par = copy(wire, pk.at[1], 4, par)
    c_par.start()
    c_sib.start()

    sources = [a, sib[1], par[1], lax.rem(sib[1] + 2, 4)]
    sub, lane = iota((ROWS, 128), 0), iota((ROWS, 128), 1)
    for d in range(4):
        count = jnp.int32(0)
        first = (t * 4 + sources[d]) * ROWS
        shift = jnp.zeros((ROWS, 128), jnp.int32)
        lows, highs = shift, shift
        for i in range(ROWS):
            start, lo, hi, length = segment(ids, first + i)
            here = sub == i
            lows = jnp.where(here, jnp.where(start, lo, 8), lows)
            highs = jnp.where(here, hi, highs)
            shift = jnp.where(here, count - lo, shift)
            count = count + jnp.where(start, hi - lo + 1, 0)
        for o in range(BAND):
            hit = jnp.logical_and(lane == shift + o, jnp.logical_and(lows <= o, highs >= o))
            sel[d, pl.ds(o * ROWS, ROWS), :] = jnp.where(hit, 1.0, 0.0).astype(BF16)

    def unpack(d, ref):
        at = pl.ds(pl.multiple_of(sources[d] * ROWS, ROWS), ROWS)
        hot = sel[d][:, :K]
        for q in range(0, Q, 2):
            w = jnp.concatenate([ref[pl.ds(q * K, K), :], ref[pl.ds((q + 1) * K, K), :]], axis=1)
            rows = dot(hot, w).astype(BF16)
            for o in range(BAND):
                out_ref[o, at, pl.ds(q * 128, 256)] = rows[o * ROWS:(o + 1) * ROWS]

    unpack(0, wire)
    c_sib.wait()
    unpack(1, pk.at[0])
    c_par.wait()
    c_fwd = copy(pk.at[1], pk.at[2], 5, sib)
    c_fwd.start()
    unpack(2, pk.at[1])
    c_fwd.wait()
    unpack(3, pk.at[2])


def run(K, cid, a_blocks, p_blocks, columns, agg_ids):
    vm = pltpu.VMEM
    out = pl.pallas_call(
        functools.partial(kernel, K),
        out_shape=jax.ShapeDtypeStruct((BAND, 4 * ROWS, BS * BS), BF16),
        in_specs=[pl.BlockSpec(memory_space=pltpu.SMEM)] * 2 + [pl.BlockSpec(memory_space=pltpu.VMEM)] * 2,
        out_specs=pl.BlockSpec(memory_space=pltpu.VMEM),
        scratch_shapes=[
            vm((Q * ROWS, 128), F32),
            vm((ROWS * Q, 128), BF16),
            vm((REACH * Q, 128), BF16),
            vm((REACH * Q, 128), BF16),
            vm((ROWS + 2 * REACH, 128, 128), BF16),
            vm((ROWS * 64, 64), BF16),
            vm((NNZB * Q * ROWS, 128), F32),
            vm((ROWS * 8 + 1, Q, 128), F32),
            vm((BAND * Q, 128), BF16),
            vm((BAND * Q, 128), BF16),
            vm((Q * K, 128), BF16),
            vm((Q * K, 128), F32),
            vm((3, Q * K, 128), BF16),
            vm((4, BAND * ROWS, 128), BF16),
            pltpu.SMEM((4, 32), jnp.int32),
            pltpu.SemaphoreType.DMA((6,)),
            pltpu.SemaphoreType.DMA((6,)),
        ],
        compiler_params=pltpu.CompilerParams(collective_id=cid, has_side_effects=True, vmem_limit_bytes=48 << 20),
    )(agg_ids, columns.T, jnp.transpose(a_blocks, (1, 0, 2)), p_blocks)
    return jnp.transpose(out, (1, 0, 2))


SLOTS = (48, 64, 112)


def most_blocks(ids):
    wide = jnp.pad(ids, (REACH, 2 * REACH), mode="edge")
    at = lambda step: lax.slice_in_dim(wide, REACH + step, REACH + step + NB)
    place = jnp.arange(NB, dtype=jnp.int32)
    start = jnp.logical_or(place == 0, at(-1) != ids)
    high = at(6)
    for length in (3, 2, 1):
        ends = jnp.logical_or(at(length) != ids, place + length >= NB)
        high = jnp.where(ends, at(length - 1 + REACH), high)
    count = jnp.where(start, high - at(-REACH) + 1, 0)
    return jnp.max(jnp.sum(count.reshape(NB // ROWS, ROWS), axis=1))


def local(a_blocks, p_blocks, columns, agg_ids):
    most = most_blocks(agg_ids)
    which = sum((most > k).astype(jnp.int32) for k in SLOTS[:-1])
    branches = [functools.partial(run, k, n) for n, k in enumerate(SLOTS)]
    return lax.switch(which, branches, a_blocks, p_blocks, columns, agg_ids)


def solution(mesh):
    return jax.shard_map(
        local,
        mesh=mesh,
        in_specs=(
            P(("tile", "agg"), None, None),
            P(("tile", "agg"), None),
            P(("tile", "agg"), None),
            P(),
        ),
        out_specs=P("tile", None, None),
        check_vma=False,
    )
```

time: 136 us -> 62 us (0.46)
  waiting for transfers between devices: 69.9 us -> 0 us
  Pallas kernels: 0 us -> 53 us
  local copies, waits for them, and re-layouts: 28 us -> 3.22 us
  starting transfers between devices: 14.1 us -> 0 us
  between operations: 14.2 us -> 1.33 us
  matrix products: 7.29 us -> 0 us
  other arithmetic: 1.63 us -> 3.23 us
    all_gather x1 -> x0, waiting for transfers between devices: 57.1 us -> none  [local(): return lax.all_gather(finished, 'agg', axis=0, tiled=True)]
    pallas_call x0 -> x1, Pallas kernels: none -> 53 us  [run(): pl.pallas_call(functools.partial(kernel, K), out_shape=jax.ShapeDtypeStru...]
    ppermute x3 -> x0, starting transfers between devices: 14 us -> none  [the longest x1 10.2 us: extended(): lax.ppermute(tail, axis, [(i, (i + 1) % count) for i in range(ends)])]
    ppermute x3 -> x0, waiting for transfers between devices: 12.8 us -> none  [the longest x1 12.3 us: shifted(): return lax.ppermute(block, axis, route)]
    dot_general x5 -> x0, matrix products: 7.29 us -> none  [the longest x1 2.28 us: local(): band_rows = jnp.einsum('iko,ikpr->iopr', select, prods).astype(jnp.bfloat16)]
    reshape x4 -> x1, local copies, waits for them, and re-layouts: 6.74 us -> 0.09 us  [most_blocks(): return jnp.max(jnp.sum(count.reshape(NB // ROWS, ROWS), axis=1))]
    dot_general x2 -> x0, local copies, waits for them, and re-layouts: 6.49 us -> none  [the longest x1 3.37 us: local(): band_rows = jnp.einsum('iko,ikpr->iopr', select, prods).astype(jnp.bfloat16)]
    transpose x1 -> x0, local copies, waits for them, and re-layouts: 3.48 us -> none  [local(): jnp.einsum('iqp,ioqr->iopr', own, band_rows, preferred_element_type=jnp.f...]
  transfers between devices with their start and end apart: 4 -> 0, of which waited for: 3 -> 0; matrix products, arithmetic and copies ran while one was open for 5% -> 0% of each run, Pallas kernels for 0% -> 0%
where the time goes in v1:
time: 62 us; the launch traced here: 61.6 us
  Pallas kernels  53 us (85%)
  other arithmetic  3.23 us (5%)
  local copies, waits for them, and re-layouts  3.22 us (5%)
  between operations  1.33 us (2%)
  loops' own time  0.74 us (1%)
    pallas_call x1, Pallas kernels, run(): pl.pallas_call(functools.partial(kernel, K), out_shape=jax.ShapeDtypeStru...  53 us
    select_n x1, other arithmetic, most_blocks(): count = jnp.where(start, high - at(-REACH) + 1, 0)  2.48 us
    unnamed x1, local copies, waits for them, and re-layouts  1.84 us
    slice x1, local copies, waits for them, and re-layouts, most_blocks(): wide = jnp.pad(ids, (REACH, 2 * REACH), mode='edge')  1.29 us

profile of v1, /device:TPU:1, one launch (start us, length us, event | category | flops | bytes accessed | tf_op | source)
XLA Modules:
  0.0 61.6 jit_solution(7552670673562510308)
XLA Ops:
  0.0 1.3 %fusion.13 = (s32[1]{0:T(128)}, s32[1]{0:T(128)}) fusion(s32[4096]{0:T(1024)} %param.10), kind=kLoop, calls=%fused_computation.25 | loop fusion | bytes 16 | tf_op jit(solution)/shard_map/jit(_pad)/slice | solution.py:256
  1.3 2.5 %fusion.3 = s32[4096]{0:T(1024)S(1)} fusion(s32[4096]{0:T(1024)} %param.10, s32[]{:T(128)} %bitcast.9, s32[]{:T(128)} %bitcast.10), kind=kLoop, calls=%fused_computation.11 | loop fusion | flops 86016 | bytes 32776 | tf_op jit(solution)/shard_map/jit(_where)/select_n | solution.py:264
  3.8 0.1 reshape.9
  3.9 0.1 reduce_sum.9
  4.0 0.6 %reduce_max.9 = s32[]{:T(128)} reduce(s32[256]{0:T(256)S(1)} %reduce_sum.9, s32[]{:T(128)} %constant.3.clone.1), dimensions={0}, to_apply=%region_1.2 | reduce | flops 255 | bytes 1032 | tf_op jit(solution)/shard_map/reduce_max | solution.py:265
  5.9 53.8 %conditional.1 = (bf16[64,7,4096]{2,0,1:T(8,128)(2,1)S(1)}) conditional(s32[]{:T(128)} %clamp.3, (s32[16,6]{0,1:T(8,128)}, bf16[16,6,4096]{2,0,1:T(8,128)(2,1)}, s32[4096]{0:T(1024)}, bf16[16,4096]{1,0:T(8,128)(2,1)}) %tuple.14, (s32[16,6]{0,1:T(8,128)}, bf16[16,6,4096]{2,0,1:T(8,128)(2,1)}, s32[4096]{0:T(1024)}, ...), branch_computations={%region_2.3_spmd, %region_3.4_spmd, %region_4.5_spmd} | conditional | bytes 8 | solution.py:272
  6.2 53.0 %branch_1_fun.1 = bf16[7,64,4096]{2,1,0:T(8,128)(2,1)S(1)} custom-call(s32[4096]{0:T(1024)} %get-tuple-element.37.ids, s32[6,16]{1,0:T(8,128)} %bitcast.18, bf16[6,16,4096]{2,1,0:T(8,128)(2,1)} %bitcast.15, bf16[16,4096]{1,0:T(8,128)(2,1)} %get-tuple-element.40.p_ref), custom_call_target="tpu_custom_call" | custom-call | tf_op jit(solution)/shard_map/cond/branch_1_fun/pallas_call | solution.py:223
  59.7 1.8 %copy.12 = bf16[64,7,4096]{2,0,1:T(8,128)(2,1)} copy(bf16[64,7,4096]{2,0,1:T(8,128)(2,1)S(1)} %get-tuple-element.45) | data formatting | bytes 7340032

commit v2 on v1

v2 whole, which is shorter than its diff:
```python
import functools

import jax
import jax.numpy as jnp
from jax import lax
from jax.experimental import pallas as pl
from jax.experimental.pallas import tpu as pltpu
from jax.sharding import PartitionSpec as P

MESH = pl.DeviceIdType.MESH
BS = 64
NNZB = 6
REACH = 3
BAND = 7
ROWS = 16
NB = 4096
Q = 32
CHUNK = 8
EARLY = 16
LAST_EARLY = 12
CLASSES = ((24, 48, 4), (32, 48, 4), (96, 96, 1))
F32 = jnp.float32
BF16 = jnp.bfloat16
I32 = jnp.int32


def dot(x, y):
    return lax.dot_general(x, y, (((1,), (0,)), ((), ())), preferred_element_type=F32)


def dot_nt(x, y):
    return lax.dot_general(x, y, (((1,), (1,)), ((), ())), preferred_element_type=F32)


def iota(shape, dim):
    return lax.broadcasted_iota(I32, shape, dim)


def choose(ids_ref, out_ref):
    ids = ids_ref[...]
    row, lane = iota((Q, 128), 0), iota((Q, 128), 1)
    flat = row * 128 + lane
    final = jnp.max(ids)

    def at(step):
        moved = pltpu.roll(ids, (-step) % 128, 1)
        other = pltpu.roll(moved, (Q - 1) if step > 0 else 1, 0)
        inside = lane + step < 128 if step > 0 else lane + step >= 0
        got = jnp.where(inside, moved, other)
        return jnp.where(flat + step >= NB, final, jnp.where(flat + step < 0, 0, got))

    start = jnp.logical_or(flat == 0, at(-1) != ids)
    high = at(6)
    length = jnp.full((Q, 128), 4, I32)
    for n in (3, 2, 1):
        ends = jnp.logical_or(at(n) != ids, flat + n >= NB)
        high = jnp.where(ends, at(n - 1 + REACH), high)
        length = jnp.where(ends, n, length)
    count = jnp.where(start, high - at(-REACH) + 1, 0)
    early = jnp.where(lax.rem(lane, ROWS) + length - 1 <= LAST_EARLY, count, 0)
    sums = (iota((128, 128), 0) // ROWS == iota((128, 128), 1)).astype(F32).astype(BF16)
    total = dot(count.astype(F32).astype(BF16), sums)
    rest = total - jnp.minimum(dot(early.astype(F32).astype(BF16), sums), float(EARLY))
    pair = jnp.where(lax.rem(lane, 2) == 0, rest + pltpu.roll(rest, 127, 1), 0.0)
    most_pair, most = jnp.max(pair).astype(I32), jnp.max(rest).astype(I32)
    which = jnp.int32(0)
    for slots, own, _ in CLASSES[:-1]:
        which = which + jnp.logical_or(most_pair > 2 * slots, most > own).astype(I32)
    out_ref[0] = which


def segment(ids, g):
    last = NB - 1
    own = ids[g]
    start = jnp.logical_or(g == 0, ids[jnp.maximum(g - 1, 0)] != own)
    length = jnp.int32(1)
    for step in range(1, 4):
        same = jnp.logical_and(g + step <= last, ids[jnp.minimum(g + step, last)] == own)
        length = length + same.astype(I32)
    low = ids[jnp.maximum(g - REACH, 0)] - own + REACH
    high = ids[jnp.minimum(g + length - 1 + REACH, last)] - own + REACH
    return start, low, high, length


def kernel(KB, KL, PH, ids, cols, a_ref, p_ref, out_ref, pscr, p2, hl, hr, dmat, lmat, ascr, blk, lead_out, lead_in,
           wa, wb, own_l, own_rows, sib_a, sib_l, sib_rows, pka, pkb, wf, sel_own, sel_a, sel_b, tab, walk, ssem, rsem):
    t = lax.axis_index("tile")
    a = lax.axis_index("agg")
    rank = t * 4 + a
    base = rank * ROWS
    ranks = NB // ROWS
    nxt = lax.rem(rank + 1, ranks)
    prv = lax.rem(rank + ranks - 1, ranks)
    dev = lambda r: (r // 4, lax.rem(r, 4))
    sib_at = a + 1 - 2 * lax.rem(a, 2)
    par_at = lax.rem(a + 2, 4)
    dia_at = lax.rem(sib_at + 2, 4)
    sib, par = (t, sib_at), (t, par_at)
    bar = pltpu.get_barrier_semaphore()
    for d in (dev(nxt), dev(prv), sib, par):
        pl.semaphore_signal(bar, inc=1, device_id=d, device_id_type=MESH)

    def copy(src, dst, n, to):
        return pltpu.make_async_remote_copy(src_ref=src, dst_ref=dst, send_sem=ssem.at[n], recv_sem=rsem.at[n], device_id=to, device_id_type=MESH)

    pf = p_ref[...].astype(F32)
    for q in range(Q):
        pscr[pl.ds(q * ROWS, ROWS), :] = pf[:, q * 128:(q + 1) * 128]
    for i in range(ROWS):
        p2[pl.ds(i * Q, Q), :] = pscr[pl.ds(i, Q, stride=ROWS), :].astype(BF16)
    pl.semaphore_wait(bar, 4)
    H = REACH * Q
    c_right = copy(p2.at[pl.ds((ROWS - REACH) * Q, H)], hl, 0, dev(nxt))
    c_left = copy(p2.at[pl.ds(0, H)], hr, 1, dev(prv))
    c_right.start()
    c_left.start()

    after, mine, mine_early = jnp.int32(ROWS), jnp.int32(0), jnp.int32(0)
    tab[0, ROWS], tab[1, ROWS], tab[2, ROWS], tab[3, ROWS] = jnp.int32(0), jnp.int32(1 << 20), jnp.int32(ROWS), jnp.int32(ROWS)
    for i in range(ROWS - 1, -1, -1):
        start, lo, hi, length = segment(ids, base + i)
        tab[0, i] = lo
        tab[1, i] = hi
        tab[2, i] = jnp.minimum(i + length - 1, ROWS - 1)
        tab[3, i] = after
        after = jnp.where(start, i, after)
        here = jnp.where(start, hi - lo + 1, 0)
        mine = mine + here
        mine_early = mine_early + jnp.where(i + length - 1 <= LAST_EARLY, here, 0)
    mine_rest = mine - jnp.minimum(mine_early, EARLY)
    s, o = after, tab[0, after]
    for m in range(EARLY + KL):
        end = tab[2, s]
        fits = end <= LAST_EARLY if m < EARLY else end >= 0
        walk[m] = jnp.where(fits, jnp.clip(end * 8 + o, 0, ROWS * 8), ROWS * 8)
        more = jnp.logical_or(o < tab[1, s], jnp.logical_not(fits))
        s2 = jnp.where(more, s, tab[3, s])
        o = jnp.where(more, o + fits.astype(I32), tab[0, s2])
        s = s2

    r_, c_ = iota((128, 64), 0), iota((128, 64), 1)
    cc = lax.rem(r_, 64)
    flip = (lax.rem(cc, 2) != r_ // 64).astype(I32)
    spread = (c_ == cc // 2 + 32 * flip).astype(F32).astype(BF16)
    diag = (iota((128, 128), 0) // 64) == (iota((128, 128), 1) // 64)
    low = iota((Q, 128), 1) < 64

    def spread_block(blockf):
        both = jnp.concatenate([blockf, pltpu.roll(blockf, 64, 1)], axis=0).astype(BF16)
        return jnp.where(diag, dot(spread, both), 0.0).astype(BF16)

    pr, pc = iota((64, 128), 0), iota((64, 128), 1)
    order = jnp.where(pr < 32, 2 * pr, 2 * (pr - 32) + 1)
    perm = (lax.rem(pc, 64) == order).astype(F32).astype(BF16)
    for i in range(ROWS):
        bf = p2[pl.ds(i * Q, Q), :].astype(F32)
        dmat[i + REACH] = spread_block(bf)
        split = jnp.concatenate([jnp.where(low, bf, 0.0), jnp.where(low, 0.0, bf)], axis=0).astype(BF16)
        lmat[pl.ds(i * 64, 64), :] = dot_nt(perm, split).astype(BF16)
    for k in range(NNZB):
        x = a_ref[k].astype(F32)
        for q in range(Q):
            ascr[pl.ds(k * 512 + q * ROWS, ROWS), :] = x[:, q * 128:(q + 1) * 128]

    def row(i, acc):
        own = ids[base + i]
        bands = [jnp.zeros((Q, 128), F32)] * 8
        for k in range(NNZB):
            a2 = ascr[pl.ds(k * 512 + i, Q, stride=ROWS), :].astype(BF16)
            j = cols[k, i]
            prod = dot(a2, dmat[jnp.clip(j - base + REACH, 0, ROWS + 2 * REACH - 1)])
            o = ids[j] - own + REACH
            for b in range(BAND):
                bands[b] = bands[b] + jnp.where(o == b, 1.0, 0.0).astype(F32) * prod
        ev, od = [], []
        for m in range(4):
            x0, x1 = bands[2 * m], bands[2 * m + 1]
            ev.append(jnp.where(low, x0, pltpu.roll(x1, 64, 1)))
            od.append(jnp.where(low, pltpu.roll(x0, 64, 1), x1))
        bcat = jnp.concatenate([jnp.concatenate(ev, axis=1), jnp.concatenate(od, axis=1)], axis=0).astype(BF16)
        term = dot(lmat[pl.ds(i * 64, 64), :], bcat)
        if acc is not None:
            term = term + jnp.where(ids[base + i - 1] == own, 1.0, 0.0).astype(F32) * acc
        for m in range(4):
            x0, y0 = term[:Q, m * 128:(m + 1) * 128], term[Q:, m * 128:(m + 1) * 128]
            blk[i * 8 + 2 * m] = jnp.where(low, x0, pltpu.roll(y0, 64, 1))
            if m < 3:
                blk[i * 8 + 2 * m + 1] = jnp.where(low, pltpu.roll(x0, 64, 1), y0)
        return term

    acc = None
    for i in range(REACH, ROWS - REACH):
        acc = row(i, acc)
    blk[ROWS * 8] = jnp.zeros((Q, 128), F32)
    c_right.wait()
    c_left.wait()
    for i in range(REACH):
        dmat[i] = spread_block(hl[pl.ds(i * Q, Q), :].astype(F32))
        dmat[i + REACH + ROWS] = spread_block(hr[pl.ds(i * Q, Q), :].astype(F32))
    first = None
    for i in range(REACH):
        first = row(i, first)

    leads = jnp.where(jnp.logical_and(base > 0, ids[jnp.maximum(base - 1, 0)] == ids[base]), 1.0, 0.0).astype(F32)
    e, run = jnp.int32(0), jnp.int32(1)
    for step in range(1, REACH):
        run = run * (ids[base + step] == ids[base]).astype(I32)
        e = e + run
    for o in range(BAND):
        lead_out[pl.ds(o * Q, Q), :] = (leads * blk[e * 8 + o]).astype(BF16)
    c_lead = copy(lead_out, lead_in, 2, dev(prv))
    c_lead.start()
    for i in range(REACH, 2 * REACH):
        joined = jnp.where(ids[base + i] == ids[base + REACH - 1], 1.0, 0.0).astype(F32)
        for o in range(BAND):
            blk[i * 8 + o] = blk[i * 8 + o] + joined * blk[(REACH - 1) * 8 + o]

    for m in range(EARLY):
        wf[pl.ds(m, Q, stride=EARLY), :] = blk[walk[m]]
    wa[...] = wf[pl.ds(0, Q * EARLY), :].astype(BF16)
    c_a_par = copy(wa, pka.at[0], 3, par)
    c_a_sib = copy(wa, sib_a, 4, sib)
    c_a_par.start()
    c_a_sib.start()

    for i in range(ROWS - REACH, ROWS):
        acc = row(i, acc)
    c_lead.wait()
    for o in range(BAND):
        at = (ROWS - 1) * 8 + o
        blk[at] = blk[at] + lead_in[pl.ds(o * Q, Q), :].astype(F32)
    for m in range(KL):
        own_l[pl.ds(m * Q, Q), :] = blk[walk[EARLY + m]].astype(BF16)
    c_l_sib = copy(own_l, sib_l, 5, sib)
    c_l_sib.start()
    c_l_sib.wait()
    for h in range(KB):
        v = own_l[pl.ds(h * Q, Q), :].astype(F32)
        m = 2 * KB - 1 - h
        if m < KL:
            v = jnp.where(h < mine_rest, v, sib_l[pl.ds(m * Q, Q), :].astype(F32))
        wf[pl.ds(h, Q, stride=KB), :] = v
    part = CHUNK * KB
    c_b = []
    for g in range(Q // CHUNK):
        at = pl.ds(g * part, part)
        wb[at, :] = wf[at, :].astype(BF16)
        c_b.append(copy(wb.at[at], pkb.at[0, at], 7 + g, par))
        c_b[-1].start()

    sub, lane = iota((ROWS, 128), 0), iota((ROWS, 128), 1)

    def places(which):
        count, early = jnp.int32(0), jnp.int32(0)
        begin = (t * 4 + which) * ROWS
        shift = jnp.zeros((ROWS, 128), I32)
        lows, highs, ends = shift, shift, shift
        for i in range(ROWS):
            start, lo, hi, length = segment(ids, begin + i)
            here = sub == i
            lows = jnp.where(here, jnp.where(start, lo, 8), lows)
            highs = jnp.where(here, hi, highs)
            shift = jnp.where(here, count - lo, shift)
            ends = jnp.where(here, i + length - 1, ends)
            more = jnp.where(start, hi - lo + 1, 0)
            count = count + more
            early = early + jnp.where(i + length - 1 <= LAST_EARLY, more, 0)
        early = jnp.minimum(early, EARLY)
        out = []
        for o in range(BAND):
            n = shift + o
            there = jnp.logical_and(lows <= o, highs >= o)
            is_early = jnp.logical_and(ends <= LAST_EARLY, n < EARLY)
            out.append((there, is_early, n, n - early))
        return out

    def hot(cond):
        return jnp.where(cond, 1.0, 0.0).astype(BF16)

    for u, which in enumerate((a, sib_at)):
        for o, (there, is_early, n, m) in enumerate(places(which)):
            col = jnp.where(is_early, n + u * EARLY, m + 2 * EARLY + u * KL)
            col = jnp.where(there, col, -1)
            for c in range(sel_own.shape[1] // 128):
                sel_own[pl.ds((o * 2 + u) * ROWS, ROWS), pl.ds(c * 128, 128)] = hot(col == lane + c * 128)
    for u, which in enumerate((par_at, dia_at)):
        for o, (there, is_early, n, m) in enumerate(places(which)):
            col_a = jnp.where(jnp.logical_and(there, is_early), n + u * PH * EARLY, -(1 << 20))
            col_b = jnp.where(m < KB, m + u * PH * KB, 2 * KB - 1 - m + (1 - u) * PH * KB)
            col_b = jnp.where(jnp.logical_and(there, jnp.logical_not(is_early)), col_b, -(1 << 20))
            for p in range(PH):
                at = pl.ds(((p * BAND + o) * 2 + u) * ROWS, ROWS)
                sel_a[at, :] = hot(col_a + p * EARLY == lane)
                for c in range(sel_b.shape[1] // 128):
                    sel_b[at, pl.ds(c * 128, 128)] = hot(col_b + p * KB == lane + c * 128)

    def put(rows, q, where):
        for o in range(BAND):
            for u in range(2):
                at = pl.ds(pl.multiple_of(where[u] * ROWS, ROWS), ROWS)
                out_ref[o, at, pl.ds(q * 128, 128)] = rows[(o * 2 + u) * ROWS:(o * 2 + u + 1) * ROWS]

    c_a_sib.wait()
    for m in range(KL):
        wf[pl.ds(m, Q, stride=KL), :] = own_l[pl.ds(m * Q, Q), :].astype(F32)
    own_rows[...] = wf[pl.ds(0, Q * KL), :].astype(BF16)
    for m in range(KL):
        wf[pl.ds(m, Q, stride=KL), :] = sib_l[pl.ds(m * Q, Q), :].astype(F32)
    sib_rows[...] = wf[pl.ds(0, Q * KL), :].astype(BF16)
    for q in range(0, Q, 2):
        two = []
        for x in (q, q + 1):
            ea, el = pl.ds(x * EARLY, EARLY), pl.ds(x * KL, KL)
            two.append(jnp.concatenate([wa[ea, :], sib_a[ea, :], own_rows[el, :], sib_rows[el, :]], axis=0))
        got = dot(sel_own[:, :2 * (EARLY + KL)], jnp.concatenate(two, axis=1)).astype(BF16)
        put(got[:, :128], q, (a, sib_at))
        put(got[:, 128:], q + 1, (a, sib_at))

    c_a_par.wait()
    c_a_fwd = copy(pka.at[0], pka.at[1], 6, sib)
    c_a_fwd.start()
    c_f = []
    for g in range(Q // CHUNK):
        at = pl.ds(g * part, part)
        c_b[g].wait()
        c_f.append(copy(pkb.at[0, at], pkb.at[1, at], 11 + g, sib))
        c_f[-1].start()
        if g == 0:
            c_a_fwd.wait()
        if g > 0:
            c_f[g - 1].wait()
            unpack_far(g - 1, PH, KB, pka, pkb, sel_a, sel_b, put, (par_at, dia_at))
    g = Q // CHUNK - 1
    c_f[g].wait()
    unpack_far(g, PH, KB, pka, pkb, sel_a, sel_b, put, (par_at, dia_at))


def unpack_far(g, PH, KB, pka, pkb, sel_a, sel_b, put, where):
    for f in range(CHUNK // (2 * PH)):
        q = g * CHUNK + f * 2 * PH
        wide_a, wide_b = [], []
        for x in (q, q + PH):
            wide_a.append(jnp.concatenate([pka[u, pl.ds(x * EARLY, PH * EARLY), :] for u in range(2)], axis=0))
            wide_b.append(jnp.concatenate([pkb[u, pl.ds(x * KB, PH * KB), :] for u in range(2)], axis=0))
        rows_a = dot(sel_a[:, :2 * PH * EARLY], jnp.concatenate(wide_a, axis=1))
        rows_b = dot(sel_b[:, :2 * PH * KB], jnp.concatenate(wide_b, axis=1))
        got = (rows_a + rows_b).astype(BF16)
        for p in range(PH):
            rows = got[p * BAND * 2 * ROWS:(p + 1) * BAND * 2 * ROWS]
            put(rows[:, :128], q + p, where)
            put(rows[:, 128:], q + PH + p, where)


def run(n, a_blocks, p_blocks, columns, agg_ids):
    KB, KL, PH = CLASSES[n]
    vm = pltpu.VMEM
    up = lambda x: -(-x // 128) * 128
    out = pl.pallas_call(
        functools.partial(kernel, KB, KL, PH),
        out_shape=jax.ShapeDtypeStruct((BAND, 4 * ROWS, BS * BS), BF16),
        in_specs=[pl.BlockSpec(memory_space=pltpu.SMEM)] * 2 + [pl.BlockSpec(memory_space=pltpu.VMEM)] * 2,
        out_specs=pl.BlockSpec(memory_space=pltpu.VMEM),
        scratch_shapes=[
            vm((Q * ROWS, 128), F32),
            vm((ROWS * Q, 128), BF16),
            vm((REACH * Q, 128), BF16),
            vm((REACH * Q, 128), BF16),
            vm((ROWS + 2 * REACH, 128, 128), BF16),
            vm((ROWS * 64, 64), BF16),
            vm((NNZB * Q * ROWS, 128), F32),
            vm((ROWS * 8 + 1, Q, 128), F32),
            vm((BAND * Q, 128), BF16),
            vm((BAND * Q, 128), BF16),
            vm((Q * EARLY, 128), BF16),
            vm((Q * KB, 128), BF16),
            vm((Q * KL, 128), BF16),
            vm((Q * KL, 128), BF16),
            vm((Q * EARLY, 128), BF16),
            vm((Q * KL, 128), BF16),
            vm((Q * KL, 128), BF16),
            vm((2, Q * EARLY, 128), BF16),
            vm((2, Q * KB, 128), BF16),
            vm((Q * max(KL, KB), 128), F32),
            vm((2 * BAND * ROWS, up(2 * (EARLY + KL))), BF16),
            vm((PH * 2 * BAND * ROWS, 128), BF16),
            vm((PH * 2 * BAND * ROWS, up(2 * PH * KB)), BF16),
            pltpu.SMEM((4, 32), I32),
            pltpu.SMEM((EARLY + KL,), I32),
            pltpu.SemaphoreType.DMA((15,)),
            pltpu.SemaphoreType.DMA((15,)),
        ],
        compiler_params=pltpu.CompilerParams(collective_id=n, has_side_effects=True, vmem_limit_bytes=48 << 20),
    )(agg_ids, columns.T, jnp.transpose(a_blocks, (1, 0, 2)), p_blocks)
    return jnp.transpose(out, (1, 0, 2))


def local(a_blocks, p_blocks, columns, agg_ids):
    which = pl.pallas_call(
        choose,
        out_shape=jax.ShapeDtypeStruct((1,), I32),
        in_specs=[pl.BlockSpec(memory_space=pltpu.VMEM)],
        out_specs=pl.BlockSpec(memory_space=pltpu.SMEM),
    )(agg_ids.reshape(Q, 128))
    branches = [functools.partial(run, n) for n in range(len(CLASSES))]
    return lax.switch(which[0], branches, a_blocks, p_blocks, columns, agg_ids)


def solution(mesh):
    return jax.shard_map(
        local,
        mesh=mesh,
        in_specs=(
            P(("tile", "agg"), None, None),
            P(("tile", "agg"), None),
            P(("tile", "agg"), None),
            P(),
        ),
        out_specs=P("tile", None, None),
        check_vma=False,
    )
```

time: 62 us -> 47.8 us (0.77)
  the two profiles are of different devices: /device:TPU:1 before, /device:TPU:71 now
where the time goes in v2:
time: 47.8 us; the launch traced here: 47.5 us
  Pallas kernels  44.3 us (93%)
  local copies, waits for them, and re-layouts  1.84 us (4%)
  loops' own time  0.69 us (1%)
  between operations  0.67 us (1%)
    pallas_call x1, Pallas kernels, run(): pl.pallas_call(functools.partial(kernel, KB, KL, PH), out_shape=jax.Shape...  42.5 us
    unnamed x1, local copies, waits for them, and re-layouts  1.84 us
    pallas_call x1, Pallas kernels, local(): pl.pallas_call(choose, out_shape=jax.ShapeDtypeStruct((1,), I32), in_spec...  1.78 us

profile of v2, /device:TPU:71, one launch (start us, length us, event | category | flops | bytes accessed | tf_op | source)
XLA Modules:
  0.0 47.5 jit_solution(3800324861464590523)
XLA Ops:
  0.0 1.8 %shard_map.58 = s32[1]{0:T(128)} custom-call(s32[32,128]{1,0:T(8,128)} %bitcast.17), custom_call_target="tpu_custom_call" | custom-call | tf_op jit(solution)/shard_map/pallas_call | solution.py:398
  2.4 43.2 %conditional.1 = (bf16[64,7,4096]{2,0,1:T(8,128)(2,1)S(1)}) conditional(s32[]{:T(128)} %bitcast.10, (s32[16,6]{0,1:T(8,128)}, bf16[16,6,4096]{2,0,1:T(8,128)(2,1)}, s32[4096]{0:T(1024)}, bf16[16,4096]{1,0:T(8,128)(2,1)}) %tuple.14, (s32[16,6]{0,1:T(8,128)}, bf16[16,6,4096]{2,0,1:T(8,128)(2,1)}, s32[4096]{0:T(1024)}, ...), branch_computations={%region_0.0_spmd, %region_1.0_spmd, %region_2.0_spmd} | conditional | bytes 8 | solution.py:405
  2.6 42.5 %branch_1_fun.1 = bf16[7,64,4096]{2,1,0:T(8,128)(2,1)S(1)} custom-call(s32[4096]{0:T(1024)} %get-tuple-element.37.ids, s32[6,16]{1,0:T(8,128)} %bitcast.19, bf16[6,16,4096]{2,1,0:T(8,128)(2,1)} %bitcast.15, bf16[16,4096]{1,0:T(8,128)(2,1)} %get-tuple-element.62.p_ref), custom_call_target="tpu_custom_call" | custom-call | tf_op jit(solution)/shard_map/cond/branch_1_fun/pallas_call | solution.py:358
  45.7 1.8 %copy.21 = bf16[64,7,4096]{2,0,1:T(8,128)(2,1)} copy(bf16[64,7,4096]{2,0,1:T(8,128)(2,1)S(1)} %get-tuple-element.45) | data formatting | bytes 7340032

commit v3 on v2

v3 whole, which is shorter than its diff:
```python
import functools

import jax
import jax.numpy as jnp
from jax import lax
from jax.experimental import pallas as pl
from jax.experimental.pallas import tpu as pltpu
from jax.sharding import PartitionSpec as P

MESH = pl.DeviceIdType.MESH
BS = 64
NNZB = 6
REACH = 3
BAND = 7
ROWS = 16
NB = 4096
Q = 32
CHUNK = 8
PARTS = ((8, 1), (8, 2), (8, 3))
EARLY = sum(f for f, _ in PARTS)
LAST = 9
NEAR = 2
CLASSES = ((16, 2), (24, 2), (112, 2))
F32 = jnp.float32
BF16 = jnp.bfloat16
I32 = jnp.int32


def dot(x, y):
    return lax.dot_general(x, y, (((1,), (0,)), ((), ())), preferred_element_type=F32)


def dot_nt(x, y):
    return lax.dot_general(x, y, (((1,), (1,)), ((), ())), preferred_element_type=F32)


def iota(shape, dim):
    return lax.broadcasted_iota(I32, shape, dim)


def level(place, length):
    end = place + length - 1
    soon = jnp.logical_and(place >= REACH, end <= LAST)
    return jnp.where(soon, 1, jnp.where(end < ROWS - REACH, 2, 3))


def choose(ids_ref, out_ref):
    ids = ids_ref[...]
    row, lane = iota((Q, 128), 0), iota((Q, 128), 1)
    flat = row * 128 + lane
    final = jnp.max(ids)

    def at(step):
        moved = pltpu.roll(ids, (-step) % 128, 1)
        other = pltpu.roll(moved, (Q - 1) if step > 0 else 1, 0)
        inside = lane + step < 128 if step > 0 else lane + step >= 0
        got = jnp.where(inside, moved, other)
        return jnp.where(flat + step >= NB, final, jnp.where(flat + step < 0, 0, got))

    start = jnp.logical_or(flat == 0, at(-1) != ids)
    high = at(6)
    length = jnp.full((Q, 128), 4, I32)
    for n in (3, 2, 1):
        ends = jnp.logical_or(at(n) != ids, flat + n >= NB)
        high = jnp.where(ends, at(n - 1 + REACH), high)
        length = jnp.where(ends, n, length)
    count = jnp.where(start, high - at(-REACH) + 1, 0)
    place = lax.rem(lane, ROWS)
    grade = level(place, length)
    sums = (iota((128, 128), 0) // ROWS == iota((128, 128), 1)).astype(F32).astype(BF16)
    upto = [jnp.where(grade <= most, count, 0).astype(F32).astype(BF16) for _, most in PARTS]
    upto = dot(jnp.concatenate(upto + [count.astype(F32).astype(BF16)], axis=0), sums)
    used = 0.0
    for n, (slots, _) in enumerate(PARTS):
        used = used + jnp.minimum(upto[n * Q:(n + 1) * Q] - used, float(slots))
    rest = upto[len(PARTS) * Q:] - used
    pair = jnp.where(lax.rem(lane, 2) == 0, rest + pltpu.roll(rest, 127, 1), 0.0)
    most = jnp.max(pair)
    which = jnp.int32(0)
    for slots, _ in CLASSES[:-1]:
        which = which + (most > float(2 * slots)).astype(I32)
    out_ref[0] = which


def segment(ids, g):
    last = NB - 1
    own = ids[g]
    start = jnp.logical_or(g == 0, ids[jnp.maximum(g - 1, 0)] != own)
    length = jnp.int32(1)
    for step in range(1, 4):
        same = jnp.logical_and(g + step <= last, ids[jnp.minimum(g + step, last)] == own)
        length = length + same.astype(I32)
    low = ids[jnp.maximum(g - REACH, 0)] - own + REACH
    high = ids[jnp.minimum(g + length - 1 + REACH, last)] - own + REACH
    return start, low, high, length


def parts_of(upto):
    ends, used = [], 0
    for n, (slots, _) in enumerate(PARTS):
        used = used + jnp.minimum(upto[n] - used, slots)
        ends.append(used)
    return ends


def kernel(KB, PH, ids_in, cols_in, a_in, p_in, out_ref, ids, cols, a_ref, p_ref, pscr, p2, hl, hr, dmat, lmat, ascr, blk, lead_out, lead_in, lead_rows, lead_mine,
           wa, sib_a, pka, wb, pkb, own_l, own_rows, sib_l, sib_rows, wf, sel_near, sel_far, tab, walk, lsem, ssem, rsem):
    KL = 2 * KB
    t = lax.axis_index("tile")
    a = lax.axis_index("agg")
    rank = t * 4 + a
    base = rank * ROWS
    ranks = NB // ROWS
    nxt = lax.rem(rank + 1, ranks)
    prv = lax.rem(rank + ranks - 1, ranks)
    dev = lambda r: (r // 4, lax.rem(r, 4))
    sib_at = a + 1 - 2 * lax.rem(a, 2)
    par_at = lax.rem(a + 2, 4)
    dia_at = lax.rem(sib_at + 2, 4)
    sib, par = (t, sib_at), (t, par_at)
    bar = pltpu.get_barrier_semaphore()
    for d in (dev(nxt), dev(prv), sib, par):
        pl.semaphore_signal(bar, inc=1, device_id=d, device_id_type=MESH)
    tiles = ranks // 4
    before = lax.rem(t + tiles - 1, tiles)

    @pl.when(a == 0)
    def _():
        for d in (lax.rem(t + 1, tiles), before):
            pl.semaphore_signal(bar, inc=1, device_id=(d, a), device_id_type=MESH)


    def copy(src, dst, n, to):
        return pltpu.make_async_remote_copy(src_ref=src, dst_ref=dst, send_sem=ssem.at[n], recv_sem=rsem.at[n], device_id=to, device_id_type=MESH)

    loads = [pltpu.make_async_copy(x, y, lsem.at[n]) for n, (x, y) in enumerate(((p_in, p_ref), (ids_in, ids), (cols_in, cols), (a_in, a_ref)))]
    for c in loads:
        c.start()
    loads[0].wait()

    pf = p_ref[...].astype(F32)
    for q in range(Q):
        pscr[pl.ds(q * ROWS, ROWS), :] = pf[:, q * 128:(q + 1) * 128]
    for i in range(ROWS):
        p2[pl.ds(i * Q, Q), :] = pscr[pl.ds(i, Q, stride=ROWS), :].astype(BF16)
    pl.semaphore_wait(bar, 4 + 2 * (a == 0).astype(I32))
    H = REACH * Q
    c_right = copy(p2.at[pl.ds((ROWS - REACH) * Q, H)], hl, 0, dev(nxt))
    c_left = copy(p2.at[pl.ds(0, H)], hr, 1, dev(prv))
    c_right.start()
    c_left.start()

    loads[1].wait()

    tab[0, ROWS], tab[1, ROWS], tab[2, ROWS], tab[3, ROWS], tab[4, ROWS] = jnp.int32(0), jnp.int32(1 << 20), jnp.int32(ROWS), jnp.int32(ROWS), jnp.int32(9)
    starts, grades = [], []
    upto = [jnp.int32(0)] * (len(PARTS) + 1)
    for i in range(ROWS):
        start, lo, hi, length = segment(ids, base + i)
        grade = level(i, length)
        starts.append(start)
        grades.append(grade)
        tab[0, i] = lo
        tab[1, i] = hi
        tab[2, i] = jnp.minimum(i + length - 1, ROWS - 1)
        tab[4, i] = grade
        here = jnp.where(start, hi - lo + 1, 0)
        for n in range(len(PARTS) + 1):
            upto[n] = upto[n] + (jnp.where(grade <= PARTS[n][1], here, 0) if n < len(PARTS) else here)
    after = jnp.int32(ROWS)
    link = [None] * ROWS
    for i in range(ROWS - 1, REACH - 1, -1):
        link[i] = after
        after = jnp.where(jnp.logical_and(starts[i], grades[i] > 1), i, after)
    for i in range(REACH - 1, -1, -1):
        link[i] = after
        after = jnp.where(starts[i], i, after)
    for i in range(ROWS - 1, REACH - 1, -1):
        soon = jnp.logical_and(starts[i], grades[i] == 1)
        link[i] = jnp.where(soon, after, link[i])
        after = jnp.where(soon, i, after)
    for i in range(ROWS):
        tab[3, i] = link[i]
    mine_rest = upto[-1] - parts_of(upto)[-1]
    s, o = after, tab[0, after]
    m = 0
    for slots, most in PARTS + ((KL, 99),):
        for _ in range(slots):
            end = tab[2, s]
            fits = tab[4, s] <= most
            walk[m] = jnp.where(fits, jnp.clip(end * 8 + o, 0, ROWS * 8), ROWS * 8)
            more = jnp.logical_or(o < tab[1, s], jnp.logical_not(fits))
            s2 = jnp.where(more, s, tab[3, s])
            o = jnp.where(more, o + fits.astype(I32), tab[0, s2])
            s = s2
            m += 1

    r_, c_ = iota((128, 64), 0), iota((128, 64), 1)
    cc = lax.rem(r_, 64)
    flip = (lax.rem(cc, 2) != r_ // 64).astype(I32)
    spread = (c_ == cc // 2 + 32 * flip).astype(F32).astype(BF16)
    diag = (iota((128, 128), 0) // 64) == (iota((128, 128), 1) // 64)
    low = iota((Q, 128), 1) < 64

    def spread_block(blockf):
        both = jnp.concatenate([blockf, pltpu.roll(blockf, 64, 1)], axis=0).astype(BF16)
        return jnp.where(diag, dot(spread, both), 0.0).astype(BF16)

    pr, pc = iota((64, 128), 0), iota((64, 128), 1)
    order = jnp.where(pr < 32, 2 * pr, 2 * (pr - 32) + 1)
    perm = (lax.rem(pc, 64) == order).astype(F32).astype(BF16)
    for i in range(ROWS):
        bf = p2[pl.ds(i * Q, Q), :].astype(F32)
        dmat[i + REACH] = spread_block(bf)
        split = jnp.concatenate([jnp.where(low, bf, 0.0), jnp.where(low, 0.0, bf)], axis=0).astype(BF16)
        lmat[pl.ds(i * 64, 64), :] = dot_nt(perm, split).astype(BF16)
    loads[2].wait()
    loads[3].wait()
    for k in range(NNZB):
        x = a_ref[k].astype(F32)
        for q in range(Q):
            ascr[pl.ds(k * 512 + q * ROWS, ROWS), :] = x[:, q * 128:(q + 1) * 128]

    def row(i, acc):
        own = ids[base + i]
        bands = [jnp.zeros((Q, 128), F32)] * 8
        for k in range(NNZB):
            a2 = ascr[pl.ds(k * 512 + i, Q, stride=ROWS), :].astype(BF16)
            j = cols[k, i]
            prod = dot(a2, dmat[jnp.clip(j - base + REACH, 0, ROWS + 2 * REACH - 1)])
            o = ids[j] - own + REACH
            for b in range(BAND):
                bands[b] = bands[b] + jnp.where(o == b, 1.0, 0.0).astype(F32) * prod
        ev, od = [], []
        for m in range(4):
            x0, x1 = bands[2 * m], bands[2 * m + 1]
            ev.append(jnp.where(low, x0, pltpu.roll(x1, 64, 1)))
            od.append(jnp.where(low, pltpu.roll(x0, 64, 1), x1))
        bcat = jnp.concatenate([jnp.concatenate(ev, axis=1), jnp.concatenate(od, axis=1)], axis=0).astype(BF16)
        term = dot(lmat[pl.ds(i * 64, 64), :], bcat)
        if acc is not None:
            term = term + jnp.where(ids[base + i - 1] == own, 1.0, 0.0).astype(F32) * acc
        for m in range(4):
            x0, y0 = term[:Q, m * 128:(m + 1) * 128], term[Q:, m * 128:(m + 1) * 128]
            blk[i * 8 + 2 * m] = jnp.where(low, x0, pltpu.roll(y0, 64, 1))
            if m < 3:
                blk[i * 8 + 2 * m + 1] = jnp.where(low, pltpu.roll(x0, 64, 1), y0)
        return term

    def early(n):
        first = sum(f for f, _ in PARTS[:n])
        slots = PARTS[n][0]
        for m in range(slots):
            wf[pl.ds(m, Q, stride=slots), :] = blk[walk[first + m]]
        wa[n] = wf[pl.ds(0, Q * slots), :].astype(BF16)
        to_par, to_sib = copy(wa.at[n], pka.at[0, n], 6 + 2 * n, par), copy(wa.at[n], sib_a.at[n], 7 + 2 * n, sib)
        to_par.start()
        to_sib.start()
        return to_par, to_sib

    blk[ROWS * 8] = jnp.zeros((Q, 128), F32)
    acc = None
    c_early = []
    for i in range(REACH, ROWS - REACH):
        acc = row(i, acc)
        if i == LAST:
            c_early.append(early(0))
    c_right.wait()
    c_left.wait()
    for i in range(REACH):
        dmat[i] = spread_block(hl[pl.ds(i * Q, Q), :].astype(F32))
        dmat[i + REACH + ROWS] = spread_block(hr[pl.ds(i * Q, Q), :].astype(F32))
    first = None
    for i in range(REACH):
        first = row(i, first)

    leads = jnp.where(jnp.logical_and(base > 0, ids[jnp.maximum(base - 1, 0)] == ids[base]), 1.0, 0.0).astype(F32)
    e, run = jnp.int32(0), jnp.int32(1)
    for step in range(1, REACH):
        run = run * (ids[base + step] == ids[base]).astype(I32)
        e = e + run
    odd = lax.rem(a, 2) == 1
    inner = jnp.where(odd, leads, 0.0)
    for o in range(BAND):
        v = blk[e * 8 + o]
        lead_out[pl.ds(o * Q, Q), :] = (inner * v).astype(BF16)
        wf[pl.ds(o, Q, stride=8), :] = leads * v
    wf[pl.ds(BAND, Q, stride=8), :] = jnp.zeros((Q, 128), F32)
    lead_mine[...] = wf[pl.ds(0, Q * 8), :].astype(BF16)
    c_lead = copy(lead_out, lead_in, 2, sib)
    c_lead.start()

    def outer(k):
        to = t if k == 0 else before
        return [pltpu.make_async_remote_copy(src_ref=lead_mine, dst_ref=lead_rows.at[k], send_sem=ssem.at[23 + n], recv_sem=rsem.at[23 + k], device_id=(to, d), device_id_type=MESH) for n, d in enumerate((0, 3))]

    for k in range(2):
        @pl.when(a == 2 - 2 * k)
        def _(k=k):
            for c in outer(k):
                c.start()

    for i in range(REACH, 2 * REACH):
        joined = jnp.where(ids[base + i] == ids[base + REACH - 1], 1.0, 0.0).astype(F32)
        for o in range(BAND):
            blk[i * 8 + o] = blk[i * 8 + o] + joined * blk[(REACH - 1) * 8 + o]

    c_early.append(early(1))
    for i in range(ROWS - REACH, ROWS):
        acc = row(i, acc)
    c_lead.wait()
    for o in range(BAND):
        at = (ROWS - 1) * 8 + o
        blk[at] = blk[at] + lead_in[pl.ds(o * Q, Q), :].astype(F32)
    c_early.append(early(2))
    for m in range(KB, KL):
        own_l[pl.ds(m * Q, Q), :] = blk[walk[EARLY + m]].astype(BF16)
    tail, body = pl.ds(KB * Q, KB * Q), pl.ds(0, KB * Q)
    c_tail = copy(own_l.at[tail], sib_l.at[tail], 3, sib)
    c_tail.start()
    for m in range(KB):
        own_l[pl.ds(m * Q, Q), :] = blk[walk[EARLY + m]].astype(BF16)
    c_body = copy(own_l.at[body], sib_l.at[body], 4, sib)
    c_body.start()
    c_tail.wait()
    for h in range(KB):
        v = own_l[pl.ds(h * Q, Q), :].astype(F32)
        v = jnp.where(h < mine_rest, v, sib_l[pl.ds((KL - 1 - h) * Q, Q), :].astype(F32))
        wf[pl.ds(h, Q, stride=KB), :] = v
    part = CHUNK * KB
    c_b = []
    for g in range(Q // CHUNK):
        at = pl.ds(g * part, part)
        wb[at, :] = wf[at, :].astype(BF16)
        c_b.append(copy(wb.at[at], pkb.at[0, at], 15 + g, par))
        c_b[-1].start()

    sub, lane = iota((ROWS, 128), 0), iota((ROWS, 128), 1)

    def places(which):
        begin = (t * 4 + which) * ROWS
        zero = jnp.zeros((ROWS, 128), I32)
        shift, lows, highs = zero, zero + 8, zero
        found = [segment(ids, begin + i) for i in range(ROWS)]
        grades = [level(i, found[i][3]) for i in range(ROWS)]
        here = [jnp.where(start, hi - lo + 1, 0) for start, lo, hi, _ in found]
        upto = [sum(jnp.where(grades[i] <= most, here[i], 0) for i in range(ROWS)) for _, most in PARTS] + [sum(here)]
        soon, later = jnp.int32(0), upto[0]
        for i in range(ROWS):
            start, lo, hi, _ = found[i]
            row_i = sub == i
            lows = jnp.where(row_i, jnp.where(start, lo, 8), lows)
            highs = jnp.where(row_i, hi, highs)
            shift = jnp.where(row_i, jnp.where(grades[i] == 1, soon, later) - lo, shift)
            soon = soon + jnp.where(grades[i] == 1, here[i], 0)
            later = later + jnp.where(grades[i] == 1, 0, here[i])
        ends = parts_of(upto)
        final = jnp.int32(0)
        for i in range(ROWS):
            final = jnp.where(found[i][0], i, final)
        final = jnp.where(lax.rem(which, 2) == 1, final, -1)
        return [(jnp.logical_and(lows <= o, highs >= o), shift + o) for o in range(BAND)], ends, final

    def build(sel, P_, pair, last, shared):
        for u, which in enumerate(pair):
            blocks, ends, final = places(which)
            for o, (there, n) in enumerate(blocks):
                m = n - ends[-1]
                if shared:
                    col = jnp.where(m < last, m + u * P_ * last, 2 * last - 1 - m + (1 - u) * P_ * last)
                else:
                    col = m + u * P_ * last
                col = col + 2 * P_ * EARLY
                step = jnp.full((ROWS, 128), last, I32)
                for k in range(len(PARTS) - 1, -1, -1):
                    slots = PARTS[k][0]
                    inside = n < ends[k]
                    begin = ends[k - 1] if k else 0
                    base_col = 2 * P_ * sum(f for f, _ in PARTS[:k]) + u * P_ * slots
                    col = jnp.where(inside, n - begin + base_col, col)
                    step = jnp.where(inside, slots, step)
                col = jnp.where(there, col, -(1 << 20))
                col2 = jnp.where(sub == final, 2 * P_ * (EARLY + last) + o, -(1 << 20))
                for p in range(P_):
                    at = pl.ds(((p * BAND + o) * 2 + u) * ROWS, ROWS)
                    for c in range(sel.shape[1] // 128):
                        sel[at, pl.ds(c * 128, 128)] = jnp.where(jnp.logical_or(col == lane + c * 128, col2 == lane + c * 128), 1.0, 0.0).astype(BF16)
                    col, col2 = col + step, col2 + 8

    def unpack(q, P_, sel, early_of, rest_of, last, where, lead):
        wide = []
        for x in (q, q + P_):
            tall = []
            for n, (slots, _) in enumerate(PARTS):
                tall += [early_of(u, n, pl.ds(x * slots, P_ * slots)) for u in range(2)]
            tall += [rest_of(u, pl.ds(x * last, P_ * last)) for u in range(2)]
            tall.append(lead_rows[lead, pl.ds(x * 8, P_ * 8), :])
            wide.append(jnp.concatenate(tall, axis=0))
        got = dot(sel[:, :2 * P_ * (EARLY + last) + 8 * P_], jnp.concatenate(wide, axis=1)).astype(BF16)
        for p in range(P_):
            for o in range(BAND):
                for u in range(2):
                    at = pl.ds(pl.multiple_of(where[u] * ROWS, ROWS), ROWS)
                    rows = got[((p * BAND + o) * 2 + u) * ROWS:((p * BAND + o) * 2 + u + 1) * ROWS]
                    out_ref[o, at, pl.ds((q + p) * 128, 128)] = rows[:, :128]
                    out_ref[o, at, pl.ds((q + P_ + p) * 128, 128)] = rows[:, 128:]

    build(sel_near, NEAR, (a, sib_at), KL, False)
    for m in range(KL):
        wf[pl.ds(m, Q, stride=KL), :] = own_l[pl.ds(m * Q, Q), :].astype(F32)
    own_rows[...] = wf[pl.ds(0, Q * KL), :].astype(BF16)
    for _, to_sib in c_early:
        to_sib.wait()
    c_body.wait()
    for m in range(KL):
        wf[pl.ds(m, Q, stride=KL), :] = sib_l[pl.ds(m * Q, Q), :].astype(F32)
    sib_rows[...] = wf[pl.ds(0, Q * KL), :].astype(BF16)
    near_early = lambda u, n, at: (wa, sib_a)[u][n, at, :]
    near_rest = lambda u, at: (own_rows, sib_rows)[u][at, :]
    c_on = []
    for n, (to_par, _) in enumerate(c_early):
        to_par.wait()
        c_on.append(copy(pka.at[0, n], pka.at[1, n], 12 + n, sib))
        c_on[-1].start()
    first_hop = [pltpu.make_async_remote_copy(src_ref=lead_mine, dst_ref=lead_rows.at[k], send_sem=ssem.at[23], recv_sem=rsem.at[23 + k], device_id=sib, device_id_type=MESH) for k in range(2)]
    second_hop = [copy(lead_rows.at[k], lead_rows.at[k], 25 + k, sib) for k in range(2)]
    ends_here = jnp.logical_or(a == 0, a == 3)

    @pl.when(ends_here)
    def _():
        for k in range(2):
            first_hop[k].wait_recv()
            second_hop[k].start()
        for k in range(2):
            second_hop[k].wait_send()

    @pl.when(jnp.logical_not(ends_here))
    def _():
        for k in range(2):
            second_hop[k].wait_recv()

    for k in range(2):
        @pl.when(a == 2 - 2 * k)
        def _(k=k):
            for c in outer(k):
                c.wait_send()

    for q in range(0, Q, 2 * NEAR):
        unpack(q, NEAR, sel_near, near_early, near_rest, KL, (a, sib_at), a // 2)

    build(sel_far, PH, (par_at, dia_at), KB, True)
    far_early = lambda u, n, at: pka[u, n, at, :]
    far_rest = lambda u, at: pkb[u, at, :]
    for c in c_on:
        c.wait()
    c_f = []
    for g in range(Q // CHUNK + 1):
        if g < Q // CHUNK:
            at = pl.ds(g * part, part)
            c_b[g].wait()
            c_f.append(copy(pkb.at[0, at], pkb.at[1, at], 19 + g, sib))
            c_f[g].start()
        if g > 0:
            c_f[g - 1].wait()
            for q in range((g - 1) * CHUNK, g * CHUNK, 2 * PH):
                unpack(q, PH, sel_far, far_early, far_rest, KB, (par_at, dia_at), 1 - a // 2)


def run(n, a_blocks, p_blocks, columns, agg_ids):
    KB, PH = CLASSES[n]
    KL = 2 * KB
    vm = pltpu.VMEM
    up = lambda x: -(-x // 128) * 128
    out = pl.pallas_call(
        functools.partial(kernel, KB, PH),
        out_shape=jax.ShapeDtypeStruct((BAND, 4 * ROWS, BS * BS), BF16),
        in_specs=[pl.BlockSpec(memory_space=pl.ANY)] * 4,
        out_specs=pl.BlockSpec(memory_space=pltpu.VMEM),
        scratch_shapes=[
            pltpu.SMEM((NB,), I32),
            pltpu.SMEM((NNZB, ROWS), I32),
            vm((NNZB, ROWS, BS * BS), BF16),
            vm((ROWS, BS * BS), BF16),
            vm((Q * ROWS, 128), F32),
            vm((ROWS * Q, 128), BF16),
            vm((REACH * Q, 128), BF16),
            vm((REACH * Q, 128), BF16),
            vm((ROWS + 2 * REACH, 128, 128), BF16),
            vm((ROWS * 64, 64), BF16),
            vm((NNZB * Q * ROWS, 128), F32),
            vm((ROWS * 8 + 1, Q, 128), F32),
            vm((BAND * Q, 128), BF16),
            vm((BAND * Q, 128), BF16),
            vm((2, Q * 8, 128), BF16),
            vm((Q * 8, 128), BF16),
            vm((len(PARTS), Q * PARTS[0][0], 128), BF16),
            vm((len(PARTS), Q * PARTS[0][0], 128), BF16),
            vm((2, len(PARTS), Q * PARTS[0][0], 128), BF16),
            vm((Q * KB, 128), BF16),
            vm((2, Q * KB, 128), BF16),
            vm((Q * KL, 128), BF16),
            vm((Q * KL, 128), BF16),
            vm((Q * KL, 128), BF16),
            vm((Q * KL, 128), BF16),
            vm((Q * KL, 128), F32),
            vm((NEAR * 2 * BAND * ROWS, up(2 * NEAR * (EARLY + KL) + 8 * NEAR)), BF16),
            vm((PH * 2 * BAND * ROWS, up(2 * PH * (EARLY + KB) + 8 * PH)), BF16),
            pltpu.SMEM((8, 32), I32),
            pltpu.SMEM((EARLY + KL,), I32),
            pltpu.SemaphoreType.DMA((4,)),
            pltpu.SemaphoreType.DMA((27,)),
            pltpu.SemaphoreType.DMA((27,)),
        ],
        compiler_params=pltpu.CompilerParams(collective_id=n, has_side_effects=True, vmem_limit_bytes=48 << 20),
    )(agg_ids, columns.T, jnp.transpose(a_blocks, (1, 0, 2)), p_blocks)
    return jnp.transpose(out, (1, 0, 2))


def local(a_blocks, p_blocks, columns, agg_ids):
    which = pl.pallas_call(
        choose,
        out_shape=jax.ShapeDtypeStruct((1,), I32),
        in_specs=[pl.BlockSpec(memory_space=pltpu.VMEM)],
        out_specs=pl.BlockSpec(memory_space=pltpu.SMEM),
    )(agg_ids.reshape(Q, 128))
    branches = [functools.partial(run, n) for n in range(len(CLASSES))]
    return lax.switch(which[0], branches, a_blocks, p_blocks, columns, agg_ids)


def solution(mesh):
    return jax.shard_map(
        local,
        mesh=mesh,
        in_specs=(
            P(("tile", "agg"), None, None),
            P(("tile", "agg"), None),
            P(("tile", "agg"), None),
            P(),
        ),
        out_specs=P("tile", None, None),
        check_vma=False,
    )
```

time: 47.8 us -> 38.8 us (0.81)
  the two profiles are of different devices: /device:TPU:71 before, /device:TPU:1 now
where the time goes in v3:
time: 38.8 us; the launch traced here: 38.6 us
  Pallas kernels  35.8 us (92%)
  local copies, waits for them, and re-layouts  1.84 us (5%)
  between operations  0.67 us (2%)
    pallas_call x1, Pallas kernels, run(): pl.pallas_call(functools.partial(kernel, KB, PH), out_shape=jax.ShapeDtyp...  34 us
    unnamed x1, local copies, waits for them, and re-layouts  1.84 us
    pallas_call x1, Pallas kernels, local(): pl.pallas_call(choose, out_shape=jax.ShapeDtypeStruct((1,), I32), in_spec...  1.78 us

profile of v3, /device:TPU:1, one launch (start us, length us, event | category | flops | bytes accessed | tf_op | source)
XLA Modules:
  0.0 38.6 jit_solution(10521021486849086038)
XLA Ops:
  0.0 1.8 %shard_map.58 = s32[1]{0:T(128)} custom-call(s32[32,128]{1,0:T(8,128)} %bitcast.17), custom_call_target="tpu_custom_call" | custom-call | tf_op jit(solution)/shard_map/pallas_call | solution.py:520
  2.4 34.4 %conditional.1 = (bf16[64,7,4096]{2,0,1:T(8,128)(2,1)S(1)}) conditional(s32[]{:T(128)} %bitcast.10, (s32[16,6]{0,1:T(8,128)}, bf16[16,6,4096]{2,0,1:T(8,128)(2,1)}, s32[4096]{0:T(1024)}, bf16[16,4096]{1,0:T(8,128)(2,1)}) %tuple.14, (s32[16,6]{0,1:T(8,128)}, bf16[16,6,4096]{2,0,1:T(8,128)(2,1)}, s32[4096]{0:T(1024)}, ...), branch_computations={%region_0.0_spmd, %region_1.0_spmd, %region_2.0_spmd} | conditional | bytes 8 | solution.py:527
  2.5 34.0 %branch_0_fun.1 = bf16[7,64,4096]{2,1,0:T(8,128)(2,1)S(1)} custom-call(s32[4096]{0:T(1024)} %get-tuple-element.32.ids_in, s32[6,16]{1,0:T(8,128)} %bitcast.18, bf16[6,16,4096]{2,1,0:T(8,128)(2,1)} %bitcast.14, bf16[16,4096]{1,0:T(8,128)(2,1)} %get-tuple-element.61.p_in), custom_call_target="tpu_custom_call" | custom-call | tf_op jit(solution)/shard_map/cond/branch_0_fun/pallas_call | solution.py:474
  36.8 1.8 %copy.21 = bf16[64,7,4096]{2,0,1:T(8,128)(2,1)} copy(bf16[64,7,4096]{2,0,1:T(8,128)(2,1)S(1)} %get-tuple-element.45) | data formatting | bytes 7340032

commit v4 on v3

--- a/solution.py
+++ b/solution.py
@@ -103,7 +103,15 @@
     return ends
 
 
-def kernel(KB, PH, ids_in, cols_in, a_in, p_in, out_ref, ids, cols, a_ref, p_ref, pscr, p2, hl, hr, dmat, lmat, ascr, blk, lead_out, lead_in, lead_rows, lead_mine,
+def each(begin, end, body):
+    if end - begin <= 64:
+        for m in range(begin, end):
+            body(m)
+    else:
+        pl.loop(begin, end)(body)
+
+
+def kernel(KB, PH, ids_in, cols_in, a_in, p_in, out_ref, ids, cols, a_ref, p_ref, pscr, p2, hl, hr, dmat, lmat, ascr, bscr, blk, lead_out, lead_in, lead_far, lead_rows,
            wa, sib_a, pka, wb, pkb, own_l, own_rows, sib_l, sib_rows, wf, sel_near, sel_far, tab, walk, lsem, ssem, rsem):
     KL = 2 * KB
     t = lax.axis_index("tile")
@@ -143,12 +151,19 @@
         pscr[pl.ds(q * ROWS, ROWS), :] = pf[:, q * 128:(q + 1) * 128]
     for i in range(ROWS):
         p2[pl.ds(i * Q, Q), :] = pscr[pl.ds(i, Q, stride=ROWS), :].astype(BF16)
-    pl.semaphore_wait(bar, 4 + 2 * (a == 0).astype(I32))
     H = REACH * Q
     c_right = copy(p2.at[pl.ds((ROWS - REACH) * Q, H)], hl, 0, dev(nxt))
     c_left = copy(p2.at[pl.ds(0, H)], hr, 1, dev(prv))
-    c_right.start()
-    c_left.start()
+
+    def meet():
+        pl.semaphore_wait(bar, 4 + 2 * (a == 0).astype(I32))
+        c_right.start()
+        c_left.start()
+
+    @pl.when(a >= 2)
+    def _():
+        meet()
+
 
     loads[1].wait()
 
@@ -182,18 +197,23 @@
     for i in range(ROWS):
         tab[3, i] = link[i]
     mine_rest = upto[-1] - parts_of(upto)[-1]
-    s, o = after, tab[0, after]
-    m = 0
+    def step(most, m, state):
+        s, o = state
+        end = tab[2, s]
+        fits = tab[4, s] <= most
+        walk[m] = jnp.where(fits, jnp.clip(end * 8 + o, 0, ROWS * 8), ROWS * 8)
+        more = jnp.logical_or(o < tab[1, s], jnp.logical_not(fits))
+        s2 = jnp.where(more, s, tab[3, s])
+        return s2, jnp.where(more, o + fits.astype(I32), tab[0, s2])
+
+    state, m = (after, tab[0, after]), 0
     for slots, most in PARTS + ((KL, 99),):
-        for _ in range(slots):
-            end = tab[2, s]
-            fits = tab[4, s] <= most
-            walk[m] = jnp.where(fits, jnp.clip(end * 8 + o, 0, ROWS * 8), ROWS * 8)
-            more = jnp.logical_or(o < tab[1, s], jnp.logical_not(fits))
-            s2 = jnp.where(more, s, tab[3, s])
-            o = jnp.where(more, o + fits.astype(I32), tab[0, s2])
-            s = s2
-            m += 1
+        if slots <= 64:
+            for _ in range(slots):
+                state = step(most, m, state)
+                m += 1
+        else:
+            state = lax.fori_loop(m, m + slots, functools.partial(step, most), state)
 
     r_, c_ = iota((128, 64), 0), iota((128, 64), 1)
     cc = lax.rem(r_, 64)
@@ -221,7 +241,7 @@
         for q in range(Q):
             ascr[pl.ds(k * 512 + q * ROWS, ROWS), :] = x[:, q * 128:(q + 1) * 128]
 
-    def row(i, acc):
+    def products(i):
         own = ids[base + i]
         bands = [jnp.zeros((Q, 128), F32)] * 8
         for k in range(NNZB):
@@ -236,16 +256,25 @@
             x0, x1 = bands[2 * m], bands[2 * m + 1]
             ev.append(jnp.where(low, x0, pltpu.roll(x1, 64, 1)))
             od.append(jnp.where(low, pltpu.roll(x0, 64, 1), x1))
-        bcat = jnp.concatenate([jnp.concatenate(ev, axis=1), jnp.concatenate(od, axis=1)], axis=0).astype(BF16)
-        term = dot(lmat[pl.ds(i * 64, 64), :], bcat)
+        bscr[i] = jnp.concatenate([jnp.concatenate(ev, axis=1), jnp.concatenate(od, axis=1)], axis=0).astype(BF16)
+
+    def row(i, acc):
+        term = dot(lmat[pl.ds(i * 64, 64), :], bscr[i])
         if acc is not None:
-            term = term + jnp.where(ids[base + i - 1] == own, 1.0, 0.0).astype(F32) * acc
+            term = term + jnp.where(ids[base + i - 1] == ids[base + i], 1.0, 0.0).astype(F32) * acc
         for m in range(4):
             x0, y0 = term[:Q, m * 128:(m + 1) * 128], term[Q:, m * 128:(m + 1) * 128]
             blk[i * 8 + 2 * m] = jnp.where(low, x0, pltpu.roll(y0, 64, 1))
             if m < 3:
                 blk[i * 8 + 2 * m + 1] = jnp.where(low, pltpu.roll(x0, 64, 1), y0)
         return term
+
+    def rows(begin, end, acc):
+        for i in range(begin, end):
+            products(i)
+        for i in range(begin, end):
+            acc = row(i, acc)
+        return acc
 
     def early(n):
         first = sum(f for f, _ in PARTS[:n])
@@ -259,40 +288,35 @@
         return to_par, to_sib
 
     blk[ROWS * 8] = jnp.zeros((Q, 128), F32)
-    acc = None
     c_early = []
-    for i in range(REACH, ROWS - REACH):
-        acc = row(i, acc)
-        if i == LAST:
-            c_early.append(early(0))
+    acc = rows(REACH, LAST + 1, None)
+
+    @pl.when(a < 2)
+    def _():
+        meet()
+
+    c_early.append(early(0))
+    acc = rows(LAST + 1, ROWS - REACH, acc)
     c_right.wait()
     c_left.wait()
     for i in range(REACH):
         dmat[i] = spread_block(hl[pl.ds(i * Q, Q), :].astype(F32))
         dmat[i + REACH + ROWS] = spread_block(hr[pl.ds(i * Q, Q), :].astype(F32))
-    first = None
-    for i in range(REACH):
-        first = row(i, first)
+    rows(0, REACH, None)
 
     leads = jnp.where(jnp.logical_and(base > 0, ids[jnp.maximum(base - 1, 0)] == ids[base]), 1.0, 0.0).astype(F32)
     e, run = jnp.int32(0), jnp.int32(1)
     for step in range(1, REACH):
         run = run * (ids[base + step] == ids[base]).astype(I32)
         e = e + run
-    odd = lax.rem(a, 2) == 1
-    inner = jnp.where(odd, leads, 0.0)
     for o in range(BAND):
-        v = blk[e * 8 + o]
-        lead_out[pl.ds(o * Q, Q), :] = (inner * v).astype(BF16)
-        wf[pl.ds(o, Q, stride=8), :] = leads * v
-    wf[pl.ds(BAND, Q, stride=8), :] = jnp.zeros((Q, 128), F32)
-    lead_mine[...] = wf[pl.ds(0, Q * 8), :].astype(BF16)
+        lead_out[pl.ds(o * Q, Q), :] = (leads * blk[e * 8 + o]).astype(BF16)
     c_lead = copy(lead_out, lead_in, 2, sib)
     c_lead.start()
 
     def outer(k):
         to = t if k == 0 else before
-        return [pltpu.make_async_remote_copy(src_ref=lead_mine, dst_ref=lead_rows.at[k], send_sem=ssem.at[23 + n], recv_sem=rsem.at[23 + k], device_id=(to, d), device_id_type=MESH) for n, d in enumerate((0, 3))]
+        return [pltpu.make_async_remote_copy(src_ref=lead_out, dst_ref=lead_far.at[k], send_sem=ssem.at[23 + n], recv_sem=rsem.at[23 + k], device_id=(to, d), device_id_type=MESH) for n, d in enumerate((0, 3))]
 
     for k in range(2):
         @pl.when(a == 2 - 2 * k)
@@ -306,27 +330,31 @@
             blk[i * 8 + o] = blk[i * 8 + o] + joined * blk[(REACH - 1) * 8 + o]
 
     c_early.append(early(1))
-    for i in range(ROWS - REACH, ROWS):
-        acc = row(i, acc)
+    rows(ROWS - REACH, ROWS, acc)
     c_lead.wait()
+    even = jnp.where(lax.rem(a, 2) == 0, 1.0, 0.0).astype(F32)
     for o in range(BAND):
         at = (ROWS - 1) * 8 + o
-        blk[at] = blk[at] + lead_in[pl.ds(o * Q, Q), :].astype(F32)
+        blk[at] = blk[at] + even * lead_in[pl.ds(o * Q, Q), :].astype(F32)
     c_early.append(early(2))
-    for m in range(KB, KL):
-        own_l[pl.ds(m * Q, Q), :] = blk[walk[EARLY + m]].astype(BF16)
+    def keep(m):
+        own_l[pl.ds(pl.multiple_of(m * Q, Q), Q), :] = blk[walk[EARLY + m]].astype(BF16)
+
+    each(KB, KL, keep)
     tail, body = pl.ds(KB * Q, KB * Q), pl.ds(0, KB * Q)
     c_tail = copy(own_l.at[tail], sib_l.at[tail], 3, sib)
     c_tail.start()
-    for m in range(KB):
-        own_l[pl.ds(m * Q, Q), :] = blk[walk[EARLY + m]].astype(BF16)
+    each(0, KB, keep)
     c_body = copy(own_l.at[body], sib_l.at[body], 4, sib)
     c_body.start()
     c_tail.wait()
-    for h in range(KB):
-        v = own_l[pl.ds(h * Q, Q), :].astype(F32)
-        v = jnp.where(h < mine_rest, v, sib_l[pl.ds((KL - 1 - h) * Q, Q), :].astype(F32))
+
+    def share(h):
+        v = own_l[pl.ds(pl.multiple_of(h * Q, Q), Q), :].astype(F32)
+        v = jnp.where(h < mine_rest, v, sib_l[pl.ds(pl.multiple_of((KL - 1 - h) * Q, Q), Q), :].astype(F32))
         wf[pl.ds(h, Q, stride=KB), :] = v
+
+    each(0, KB, share)
     part = CHUNK * KB
     c_b = []
     for g in range(Q // CHUNK):
@@ -406,14 +434,15 @@
                     out_ref[o, at, pl.ds((q + P_ + p) * 128, 128)] = rows[:, 128:]
 
     build(sel_near, NEAR, (a, sib_at), KL, False)
-    for m in range(KL):
-        wf[pl.ds(m, Q, stride=KL), :] = own_l[pl.ds(m * Q, Q), :].astype(F32)
+    def lay(ref, m):
+        wf[pl.ds(m, Q, stride=KL), :] = ref[pl.ds(pl.multiple_of(m * Q, Q), Q), :].astype(F32)
+
+    each(0, KL, functools.partial(lay, own_l))
     own_rows[...] = wf[pl.ds(0, Q * KL), :].astype(BF16)
     for _, to_sib in c_early:
         to_sib.wait()
     c_body.wait()
-    for m in range(KL):
-        wf[pl.ds(m, Q, stride=KL), :] = sib_l[pl.ds(m * Q, Q), :].astype(F32)
+    each(0, KL, functools.partial(lay, sib_l))
     sib_rows[...] = wf[pl.ds(0, Q * KL), :].astype(BF16)
     near_early = lambda u, n, at: (wa, sib_a)[u][n, at, :]
     near_rest = lambda u, at: (own_rows, sib_rows)[u][at, :]
@@ -422,8 +451,8 @@
         to_par.wait()
         c_on.append(copy(pka.at[0, n], pka.at[1, n], 12 + n, sib))
         c_on[-1].start()
-    first_hop = [pltpu.make_async_remote_copy(src_ref=lead_mine, dst_ref=lead_rows.at[k], send_sem=ssem.at[23], recv_sem=rsem.at[23 + k], device_id=sib, device_id_type=MESH) for k in range(2)]
-    second_hop = [copy(lead_rows.at[k], lead_rows.at[k], 25 + k, sib) for k in range(2)]
+    first_hop = [pltpu.make_async_remote_copy(src_ref=lead_out, dst_ref=lead_far.at[k], send_sem=ssem.at[23], recv_sem=rsem.at[23 + k], device_id=sib, device_id_type=MESH) for k in range(2)]
+    second_hop = [copy(lead_far.at[k], lead_far.at[k], 25 + k, sib) for k in range(2)]
     ends_here = jnp.logical_or(a == 0, a == 3)
 
     @pl.when(ends_here)
@@ -445,6 +474,11 @@
             for c in outer(k):
                 c.wait_send()
 
+    for k in range(2):
+        for o in range(BAND):
+            wf[pl.ds(o, Q, stride=8), :] = lead_far[k, pl.ds(o * Q, Q), :].astype(F32)
+        wf[pl.ds(BAND, Q, stride=8), :] = jnp.zeros((Q, 128), F32)
+        lead_rows[k] = wf[pl.ds(0, Q * 8), :].astype(BF16)
     for q in range(0, Q, 2 * NEAR):
         unpack(q, NEAR, sel_near, near_early, near_rest, KL, (a, sib_at), a // 2)
 
@@ -488,11 +522,12 @@
             vm((ROWS + 2 * REACH, 128, 128), BF16),
             vm((ROWS * 64, 64), BF16),
             vm((NNZB * Q * ROWS, 128), F32),
+            vm((ROWS, 64, 512), BF16),
             vm((ROWS * 8 + 1, Q, 128), F32),
             vm((BAND * Q, 128), BF16),
             vm((BAND * Q, 128), BF16),
+            vm((2, BAND * Q, 128), BF16),
             vm((2, Q * 8, 128), BF16),
-            vm((Q * 8, 128), BF16),
             vm((len(PARTS), Q * PARTS[0][0], 128), BF16),
             vm((len(PARTS), Q * PARTS[0][0], 128), BF16),
             vm((2, len(PARTS), Q * PARTS[0][0], 128), BF16),

time: 38.8 us -> 40.7 us (1.049)
  the two profiles are of different devices: /device:TPU:1 before, /device:TPU:65 now
where the time goes in v4:
time: 40.7 us; the launch traced here: 40.5 us
  Pallas kernels  37.5 us (92%)
  local copies, waits for them, and re-layouts  1.84 us (5%)
  between operations  0.67 us (2%)
  loops' own time  0.51 us (1%)
    pallas_call x1, Pallas kernels, run(): pl.pallas_call(functools.partial(kernel, KB, PH), out_shape=jax.ShapeDtyp...  35.7 us
    unnamed x1, local copies, waits for them, and re-layouts  1.84 us
    pallas_call x1, Pallas kernels, local(): pl.pallas_call(choose, out_shape=jax.ShapeDtypeStruct((1,), I32), in_spec...  1.78 us

profile of v4, /device:TPU:65, one launch (start us, length us, event | category | flops | bytes accessed | tf_op | source)
XLA Modules:
  0.0 40.5 jit_solution(5704920076487262341)
XLA Ops:
  0.0 1.8 %shard_map.58 = s32[1]{0:T(128)} custom-call(s32[32,128]{1,0:T(8,128)} %bitcast.17), custom_call_target="tpu_custom_call" | custom-call | tf_op jit(solution)/shard_map/pallas_call | solution.py:555
  2.4 36.2 %conditional.1 = (bf16[64,7,4096]{2,0,1:T(8,128)(2,1)S(1)}) conditional(s32[]{:T(128)} %bitcast.10, (s32[16,6]{0,1:T(8,128)}, bf16[16,6,4096]{2,0,1:T(8,128)(2,1)}, s32[4096]{0:T(1024)}, bf16[16,4096]{1,0:T(8,128)(2,1)}) %tuple.14, (s32[16,6]{0,1:T(8,128)}, bf16[16,6,4096]{2,0,1:T(8,128)(2,1)}, s32[4096]{0:T(1024)}, ...), branch_computations={%region_0.0_spmd, %region_1.0_spmd, %region_2.0_spmd} | conditional | bytes 8 | solution.py:562
  2.5 35.7 %branch_1_fun.1 = bf16[7,64,4096]{2,1,0:T(8,128)(2,1)S(1)} custom-call(s32[4096]{0:T(1024)} %get-tuple-element.37.ids_in, s32[6,16]{1,0:T(8,128)} %bitcast.19, bf16[6,16,4096]{2,1,0:T(8,128)(2,1)} %bitcast.15, bf16[16,4096]{1,0:T(8,128)(2,1)} %get-tuple-element.62.p_in), custom_call_target="tpu_custom_call" | custom-call | tf_op jit(solution)/shard_map/cond/branch_1_fun/pallas_call | solution.py:508
  38.7 1.8 %copy.21 = bf16[64,7,4096]{2,0,1:T(8,128)(2,1)} copy(bf16[64,7,4096]{2,0,1:T(8,128)(2,1)S(1)} %get-tuple-element.45) | data formatting | bytes 7340032

commit v5 on v4

--- a/solution.py
+++ b/solution.py
@@ -282,21 +282,25 @@
         for m in range(slots):
             wf[pl.ds(m, Q, stride=slots), :] = blk[walk[first + m]]
         wa[n] = wf[pl.ds(0, Q * slots), :].astype(BF16)
-        to_par, to_sib = copy(wa.at[n], pka.at[0, n], 6 + 2 * n, par), copy(wa.at[n], sib_a.at[n], 7 + 2 * n, sib)
-        to_par.start()
-        to_sib.start()
-        return to_par, to_sib
+        for c in c_early[n]:
+            c.start()
+
+    c_early = [(copy(wa.at[n], pka.at[0, n], 6 + 2 * n, par), copy(wa.at[n], sib_a.at[n], 7 + 2 * n, sib)) for n in range(len(PARTS))]
 
     blk[ROWS * 8] = jnp.zeros((Q, 128), F32)
-    c_early = []
     acc = rows(REACH, LAST + 1, None)
+
+    @pl.when(a >= 2)
+    def _():
+        early(0)
+
+    acc = rows(LAST + 1, ROWS - REACH, acc)
 
     @pl.when(a < 2)
     def _():
         meet()
-
-    c_early.append(early(0))
-    acc = rows(LAST + 1, ROWS - REACH, acc)
+        early(0)
+
     c_right.wait()
     c_left.wait()
     for i in range(REACH):
@@ -329,14 +333,14 @@
         for o in range(BAND):
             blk[i * 8 + o] = blk[i * 8 + o] + joined * blk[(REACH - 1) * 8 + o]
 
-    c_early.append(early(1))
+    early(1)
     rows(ROWS - REACH, ROWS, acc)
     c_lead.wait()
     even = jnp.where(lax.rem(a, 2) == 0, 1.0, 0.0).astype(F32)
     for o in range(BAND):
         at = (ROWS - 1) * 8 + o
         blk[at] = blk[at] + even * lead_in[pl.ds(o * Q, Q), :].astype(F32)
-    c_early.append(early(2))
+    early(2)
     def keep(m):
         own_l[pl.ds(pl.multiple_of(m * Q, Q), Q), :] = blk[walk[EARLY + m]].astype(BF16)
 
@@ -479,25 +483,25 @@
             wf[pl.ds(o, Q, stride=8), :] = lead_far[k, pl.ds(o * Q, Q), :].astype(F32)
         wf[pl.ds(BAND, Q, stride=8), :] = jnp.zeros((Q, 128), F32)
         lead_rows[k] = wf[pl.ds(0, Q * 8), :].astype(BF16)
-    for q in range(0, Q, 2 * NEAR):
-        unpack(q, NEAR, sel_near, near_early, near_rest, KL, (a, sib_at), a // 2)
-
     build(sel_far, PH, (par_at, dia_at), KB, True)
+
+    c_f = []
+    for g in range(Q // CHUNK):
+        for q in range(g * CHUNK, (g + 1) * CHUNK, 2 * NEAR):
+            unpack(q, NEAR, sel_near, near_early, near_rest, KL, (a, sib_at), a // 2)
+        at = pl.ds(g * part, part)
+        c_b[g].wait()
+        c_f.append(copy(pkb.at[0, at], pkb.at[1, at], 19 + g, sib))
+        c_f[g].start()
+
     far_early = lambda u, n, at: pka[u, n, at, :]
     far_rest = lambda u, at: pkb[u, at, :]
     for c in c_on:
         c.wait()
-    c_f = []
-    for g in range(Q // CHUNK + 1):
-        if g < Q // CHUNK:
-            at = pl.ds(g * part, part)
-            c_b[g].wait()
-            c_f.append(copy(pkb.at[0, at], pkb.at[1, at], 19 + g, sib))
-            c_f[g].start()
-        if g > 0:
-            c_f[g - 1].wait()
-            for q in range((g - 1) * CHUNK, g * CHUNK, 2 * PH):
-                unpack(q, PH, sel_far, far_early, far_rest, KB, (par_at, dia_at), 1 - a // 2)
+    for g in range(Q // CHUNK):
+        c_f[g].wait()
+        for q in range(g * CHUNK, (g + 1) * CHUNK, 2 * PH):
+            unpack(q, PH, sel_far, far_early, far_rest, KB, (par_at, dia_at), 1 - a // 2)
 
 
 def run(n, a_blocks, p_blocks, columns, agg_ids):

time: 40.7 us -> 40.7 us (level)
  no operation moved by 1% of the time
where the time goes in v5:
time: 40.7 us; the launch traced here: 40.6 us
  Pallas kernels  37.5 us (92%)
  local copies, waits for them, and re-layouts  1.84 us (5%)
  between operations  0.67 us (2%)
  loops' own time  0.51 us (1%)
    pallas_call x1, Pallas kernels, run(): pl.pallas_call(functools.partial(kernel, KB, PH), out_shape=jax.ShapeDtyp...  35.8 us
    unnamed x1, local copies, waits for them, and re-layouts  1.84 us
    pallas_call x1, Pallas kernels, local(): pl.pallas_call(choose, out_shape=jax.ShapeDtypeStruct((1,), I32), in_spec...  1.78 us

profile of v5, /device:TPU:65, one launch (start us, length us, event | category | flops | bytes accessed | tf_op | source)
XLA Modules:
  0.0 40.6 jit_solution(4031649542832226655)
XLA Ops:
  0.0 1.8 %shard_map.58 = s32[1]{0:T(128)} custom-call(s32[32,128]{1,0:T(8,128)} %bitcast.17), custom_call_target="tpu_custom_call" | custom-call | tf_op jit(solution)/shard_map/pallas_call | solution.py:559
  2.4 36.3 %conditional.1 = (bf16[64,7,4096]{2,0,1:T(8,128)(2,1)S(1)}) conditional(s32[]{:T(128)} %bitcast.10, (s32[16,6]{0,1:T(8,128)}, bf16[16,6,4096]{2,0,1:T(8,128)(2,1)}, s32[4096]{0:T(1024)}, bf16[16,4096]{1,0:T(8,128)(2,1)}) %tuple.14, (s32[16,6]{0,1:T(8,128)}, bf16[16,6,4096]{2,0,1:T(8,128)(2,1)}, s32[4096]{0:T(1024)}, ...), branch_computations={%region_0.0_spmd, %region_1.0_spmd, %region_2.0_spmd} | conditional | bytes 8 | solution.py:566
  2.5 35.8 %branch_1_fun.1 = bf16[7,64,4096]{2,1,0:T(8,128)(2,1)S(1)} custom-call(s32[4096]{0:T(1024)} %get-tuple-element.37.ids_in, s32[6,16]{1,0:T(8,128)} %bitcast.19, bf16[6,16,4096]{2,1,0:T(8,128)(2,1)} %bitcast.15, bf16[16,4096]{1,0:T(8,128)(2,1)} %get-tuple-element.62.p_in), custom_call_target="tpu_custom_call" | custom-call | tf_op jit(solution)/shard_map/cond/branch_1_fun/pallas_call | solution.py:512
  38.7 1.8 %copy.21 = bf16[64,7,4096]{2,0,1:T(8,128)(2,1)} copy(bf16[64,7,4096]{2,0,1:T(8,128)(2,1)S(1)} %get-tuple-element.45) | data formatting | bytes 7340032
